TPU v7x, 128 devices: a whole 4x4x4 slice. The times are simulated.
128 devices in a mesh: dp: 16 (over z, y_hi, core), seq: 8 (over y_lo, x).
Axes of the slice: x: 4, y: 4 (y_hi: 2, y_lo: 2; y = y_hi * 2 + y_lo), z: 4, core: 2. Of those that a mesh axis runs over, the one named last changes fastest.
Arguments:
- tokens: bfloat16 [16, 2048, 640], P('dp', 'seq'), may hold values from -6 to 6
- positions: int32 [16, 2048], P('dp', 'seq'), may hold values from 0 to 1790, as said below
- w_query: bfloat16 [640, 1024], P(('dp', 'seq')), may hold values from -0.25 to 0.25
- w_key: bfloat16 [640, 256], P(('dp', 'seq')), may hold values from -0.25 to 0.25
- w_value: bfloat16 [640, 256], P(('dp', 'seq')), may hold values from -0.25 to 0.25
- w_out: bfloat16 [1024, 640], P(('dp', 'seq')), may hold values from -0.1875 to 0.1875
- w_gate: bfloat16 [640, 2048], P(('dp', 'seq')), may hold values from -0.25 to 0.25
- w_up: bfloat16 [640, 2048], P(('dp', 'seq')), may hold values from -0.25 to 0.25
- w_down: bfloat16 [2048, 640], P(('dp', 'seq')), may hold values from -0.125 to 0.125
- norm_input: bfloat16 [640], P(('dp', 'seq')), may hold values from -0.3984375 to 0.3984375
- norm_post_attn: bfloat16 [640], P(('dp', 'seq')), may hold values from -0.3984375 to 0.3984375
- norm_pre_ff: bfloat16 [640], P(('dp', 'seq')), may hold values from -0.3984375 to 0.3984375
- norm_post_ff: bfloat16 [640], P(('dp', 'seq')), may hold values from -0.3984375 to 0.3984375
- norm_query: bfloat16 [256], P(('dp', 'seq')), may hold values from -0.3984375 to 0.3984375
- norm_key: bfloat16 [256], P(('dp', 'seq')), may hold values from -0.3984375 to 0.3984375
- cotangent: bfloat16 [16, 2048, 640], P('dp', 'seq'), may hold values from -6 to 6
Outputs:
- mixed: bfloat16 [16, 2048, 640], P('dp', 'seq')
- grad_tokens: bfloat16 [16, 2048, 640], P('dp', 'seq')
- grad_w_query: float32 [640, 1024], P(('dp', 'seq'))
- grad_w_key: float32 [640, 256], P(('dp', 'seq'))
- grad_w_value: float32 [640, 256], P(('dp', 'seq'))
- grad_w_out: float32 [1024, 640], P(('dp', 'seq'))
- grad_w_gate: float32 [640, 2048], P(('dp', 'seq'))
- grad_w_up: float32 [640, 2048], P(('dp', 'seq'))
- grad_w_down: float32 [2048, 640], P(('dp', 'seq'))
- grad_norm_input: float32 [640], P(('dp', 'seq'))
- grad_norm_post_attn: float32 [640], P(('dp', 'seq'))
- grad_norm_pre_ff: float32 [640], P(('dp', 'seq'))
- grad_norm_post_ff: float32 [640], P(('dp', 'seq'))
- grad_norm_query: float32 [256], P(('dp', 'seq'))
- grad_norm_key: float32 [256], P(('dp', 'seq'))
Inputs may be any that keep to these rules, and one draw needn't show every extreme that they name: Each sequence holds three documents laid end to end; positions count up by one from 0 within each; the first and the last document hold 1 to 256 tokens each and 257 tokens together, so the middle one holds 1791.
All inputs are finite; a program needn't handle non-finite values.
Results may differ from a plain program's by a relative error of at most 0.025.
Values may be sent and summed in bfloat16 or wider, within the bound.
No kernel may reach another device: no remote copies, remote signals or barrier semaphores. Data moves between devices by JAX's collectives and lax.ppermute only.
A program may use at most 192 MiB of HBM per device.

v0:
```python
import functools

import jax
import jax.numpy as jnp
import numpy as np
from jax import lax
from jax.experimental import pallas as pl
from jax.experimental.pallas import tpu as pltpu
from jax.sharding import Mesh, PartitionSpec as P

EPS = 1e-06
BELOW = -1e30
WINDOW = 512
ROOT = 0.7978845608028654
CUBE = 0.044715
SIZES = (("z", 4), ("yh", 2), ("core", 2), ("yl", 2), ("x", 4))
AXES = tuple(name for name, _ in SIZES)
DP, SEQ = (AXES[:3], AXES[3:])
NEAR_Z = ("yh", "core", "yl", "x")
NEAR_Y = ("z", "core", "x")
Y = ("yh", "yl")
SWAP = ((0, 1), (1, 0))
GAINS = (5, 5, 5, 5, 2, 2)
BF, F32 = (jnp.bfloat16, jnp.float32)

ROWS = 160
GATE_AT, UP_AT = (768, 2048)


def dot(a, b):
    return jnp.dot(a, b, preferred_element_type=F32)


def dot_tn(a, b):
    return lax.dot_general(a, b, (((0,), (0,)), ((), ())), preferred_element_type=F32)


def dot_nt(a, b):
    return lax.dot_general(a, b, (((1,), (1,)), ((), ())), preferred_element_type=F32)


def panels(ref, base, count, rows):
    return jnp.concatenate(
        [
            jnp.concatenate([ref[z, pl.ds(base + p * rows, rows), :] for z in range(4)], axis=0)
            for p in range(count)
        ],
        axis=1,
    )


def columns(ref, begin, count):
    return jnp.concatenate([ref[p * 640 : (p + 1) * 640, :] for p in range(begin, begin + count)], axis=1)


def put_panels(ref, base, value, rows):
    for p in range(value.shape[1] // 128):
        for z in range(4):
            ref[z, base + p * rows : base + (p + 1) * rows, :] = value[
                z * rows : (z + 1) * rows, p * 128 : (p + 1) * 128
            ].astype(ref.dtype)


def rms(v, gain):
    return v * lax.rsqrt(jnp.mean(v * v, axis=-1, keepdims=True) + EPS) * (1.0 + gain)


def rms_back(v, gain, dy):
    r = lax.rsqrt(jnp.mean(v * v, axis=-1, keepdims=True) + EPS)
    n = v * r
    dn = dy * (1.0 + gain)
    dv = r * (dn - n * jnp.mean(dn * n, axis=-1, keepdims=True))
    return dv, jnp.sum(dy * n, axis=0, keepdims=True)


def turn(v, c, s):
    a, b = (v[:, :128], v[:, 128:])
    return jnp.concatenate([a * c - b * s, b * c + a * s], axis=1)


def turn_back(d, c, s):
    a, b = (d[:, :128], d[:, 128:])
    return jnp.concatenate([a * c + b * s, b * c - a * s], axis=1)


def owner_mask(width, per):
    d = lax.broadcasted_iota(jnp.int32, (128, width), 0) * per
    j = lax.broadcasted_iota(jnp.int32, (128, width), 1)
    return (j >= d) & (j < d + per)


def allowed_pairs(pos_ref):
    i = lax.broadcasted_iota(jnp.int32, (256, 768), 0)
    j = lax.broadcasted_iota(jnp.int32, (256, 768), 1)
    distance = 512 + i - j
    return (distance >= 0) & (distance <= jnp.minimum(pos_ref[...], WINDOW - 1))


def attend_kernel(
    core_ref, x0, x1, x2, own, oth, cos_ref, sin_ref, pos_ref, m5, m2,
    normed_ref, qraw_ref, kraw_ref, q_ref, kv_ref, gain_ref, att_ref, log_ref,
):
    first = core_ref[0] == 0
    table = own[3840:3968, :]
    wide = dot_tn(table, owner_mask(640, 5).astype(BF))
    thin = dot_tn(table, owner_mask(256, 2).astype(BF))
    lane5 = lax.broadcasted_iota(jnp.int32, (128, 640), 0)
    lane2 = lax.broadcasted_iota(jnp.int32, (128, 256), 0)
    gains = [
        jnp.sum(jnp.where(lane5 == m5[...] + 5 * n, wide, 0.0), axis=0, keepdims=True) for n in range(4)
    ]
    heads = [
        jnp.sum(jnp.where(lane2 == m2[...] + 20 + 2 * n, thin, 0.0), axis=0, keepdims=True) for n in range(2)
    ]
    pad = jnp.zeros((1, 384), F32)
    for n in range(4):
        gain_ref[n : n + 1, :] = gains[n]
    for n in range(2):
        gain_ref[4 + n : 5 + n, :] = jnp.concatenate([heads[n], pad], axis=1)
    gain_ref[6:8, :] = jnp.zeros((2, 640), F32)
    for n, ref in enumerate((x2, x1, x0)):
        normed_ref[n * 256 : (n + 1) * 256, :] = rms(ref[...].astype(F32), gains[0]).astype(BF)
    normed = normed_ref[...]
    c, s = (cos_ref[...], sin_ref[...])
    kv_own, kv_oth = [dot(normed, columns(ref, 4, 2)) for ref in (own, oth)]
    left, right = (jnp.where(first, kv_own, kv_oth), jnp.where(first, kv_oth, kv_own))
    kraw = jnp.concatenate([left[:, :128], right[:, :128]], axis=1)
    kraw_ref[...] = kraw
    keys = turn(rms(kraw, heads[1]), c, s).astype(BF)
    values = jnp.concatenate([left[:, 128:], right[:, 128:]], axis=1).astype(BF)
    kv_ref[:, :256] = keys
    kv_ref[:, 256:] = values
    c, s = (c[512:], s[512:])
    allowed = allowed_pairs(pos_ref)
    for side, ref in enumerate((own, oth)):
        raw = dot(normed_ref[512:, :], columns(ref, 0, 4))
        for h in range(2):
            slot = 2 * side + h
            one = raw[:, h * 256 : (h + 1) * 256]
            qraw_ref[slot] = one
            q = turn(rms(one, heads[0]), c, s).astype(BF)
            q_ref[slot] = q
            scores = jnp.where(allowed, dot_nt(q, keys) * 0.0625, BELOW)
            top = jnp.max(scores, axis=-1, keepdims=True)
            exps = jnp.exp(scores - top)
            total = jnp.sum(exps, axis=-1, keepdims=True)
            att_ref[slot] = dot((exps / total).astype(BF), values).astype(BF)
            log_ref[slot] = jnp.broadcast_to(top + jnp.log(total), (256, 128))


def gelu_parts(x):
    t = jnp.tanh(ROOT * (x + CUBE * x * x * x))
    half = 0.5 * (1.0 + t)
    return x * half, half + 0.5 * x * (1.0 - t * t) * ROOT * (1.0 + 3.0 * CUBE * x * x)


def feed_kernel(
    core_ref, x_ref, g_ref, att_ref, gain_ref, own, oth, down_own, down_oth,
    mixed_ref, dhid_ref, datt_ref, dgain_ref, gff_own, gff_oth, gx_own, gx_oth,
):
    core = core_ref[0]
    first = core == 0
    gain_pa, gain_pf, gain_po = [gain_ref[n : n + 1, :] for n in (1, 2, 3)]

    def join(a, b):
        return jnp.where(
            first, jnp.concatenate([a, b[:, 128:]], axis=1), jnp.concatenate([b[:, :256], a], axis=1)
        )

    def part(v):
        low, high = (v[:, :384], v[:, 256:])
        own, oth = (jnp.where(first, low, high), jnp.where(first, high, low))
        lanes = lax.broadcasted_iota(jnp.int32, oth.shape, 1)
        begin = jnp.where(first, 0, 256)
        once = jnp.where((lanes >= begin) & (lanes < begin + 128), 0.0, oth)
        return own.astype(BF), oth.astype(BF), once.astype(BF)

    def out_panels(ref, slot):
        block = lax.rem(slot + 2 * core, 4)
        return jnp.concatenate([ref[block, p * 256 : (p + 1) * 256, :] for p in range(3)], axis=1)

    out_own = [out_panels(own, s) for s in range(4)]
    out_oth = [out_panels(oth, s) for s in range(4)]
    a = sum(dot(att_ref[s], out_own[s]) for s in range(4))
    b = sum(dot(att_ref[s], out_oth[s]) for s in range(4))
    branch = join(a, b)
    hidden = x_ref[...].astype(F32) + rms(branch, gain_pa)
    ff = rms(hidden, gain_pf).astype(BF)

    def down_rows(ref, hand):
        begin = lax.rem(core + hand, 2) * 64
        return jnp.concatenate(
            [ref[pl.ds(begin, 64), p * 16 : (p + 1) * 16].reshape(1024, 128) for p in range(3)], axis=1
        )

    gates = [panels(ref, GATE_AT, 8, ROWS) for ref in (own, oth)]
    ups = [panels(ref, UP_AT, 8, ROWS) for ref in (own, oth)]
    kept = []
    a = b = 0.0
    for hand in range(2):
        gate, up = (dot(ff, gates[hand]), dot(ff, ups[hand]))
        gelu, slope = gelu_parts(gate)
        product = (gelu * up).astype(BF)
        kept.append((up * slope, gelu, product))
        a = a + dot(product, down_rows(down_own, hand))
        b = b + dot(product, down_rows(down_oth, hand))
    ff_out = join(a, b)
    mixed_ref[...] = (hidden + rms(ff_out, gain_po)).astype(BF)

    g = g_ref[...].astype(F32)
    d_ff_out, d_po = rms_back(ff_out, gain_po, g)
    d_own, d_oth, d_oth_once = part(d_ff_out)
    d_in = 0.0
    for hand in range(2):
        slope, gelu, product = kept[hand]
        begin = lax.rem(core + hand, 2) * 64
        for ref, d in ((gx_own, d_own), (gx_oth, d_oth)):
            grad = dot_tn(product, d).astype(BF)
            for p in range(3):
                cut = grad[:, p * 128 : (p + 1) * 128].reshape(64, 16, 128)
                ref[pl.ds(begin, 64), p * 16 : (p + 1) * 16] = cut
        d_product = dot_nt(d_own, down_rows(down_own, hand)) + dot_nt(d_oth_once, down_rows(down_oth, hand))
        d_gate, d_up = ((d_product * slope).astype(BF), (d_product * gelu).astype(BF))
        ref = (gff_own, gff_oth)[hand]
        put_panels(ref, 0, dot_tn(ff, d_gate), ROWS)
        put_panels(ref, UP_AT - GATE_AT, dot_tn(ff, d_up), ROWS)
        d_in = d_in + dot_nt(d_gate, gates[hand]) + dot_nt(d_up, ups[hand])
    d_hidden, d_pf = rms_back(hidden, gain_pf, d_in)
    d_hidden = d_hidden + g
    dhid_ref[...] = d_hidden
    d_branch, d_pa = rms_back(branch, gain_pa, d_hidden)
    d_own, d_oth, d_oth_once = part(d_branch)
    for s in range(4):
        block = lax.rem(s + 2 * core, 4)
        for ref, d in ((gx_own, d_own), (gx_oth, d_oth)):
            grad = dot_tn(att_ref[s], d)
            cut = [grad[:, p * 128 : (p + 1) * 128].reshape(32, 8, 128) for p in range(3)]
            cut.append(jnp.zeros_like(cut[0]))
            for pair in range(2):
                rows = jnp.concatenate(cut[2 * pair : 2 * pair + 2], axis=1)
                ref[pl.ds(block * 32, 32), 48 + pair * 16 : 64 + pair * 16] = rows.astype(BF)
        datt_ref[s] = (dot_nt(d_own, out_own[s]) + dot_nt(d_oth_once, out_oth[s])).astype(BF)
    dgain_ref[0:1, :] = d_pa
    dgain_ref[1:2, :] = d_pf
    dgain_ref[2:3, :] = d_po
    dgain_ref[3:8, :] = jnp.zeros((5, 640), F32)


def attend_back_kernel(q_ref, kv_ref, pos_ref, log_ref, datt_ref, dq_ref, dkv_ref):
    keys, values = (kv_ref[:, :256], kv_ref[:, 256:])
    allowed = allowed_pairs(pos_ref)
    dk = dv = 0.0
    for h in range(4):
        q, d_att = (q_ref[h], datt_ref[h])
        scores = jnp.where(allowed, dot_nt(q, keys) * 0.0625, BELOW)
        probs = jnp.exp(scores - log_ref[h][:, :1])
        dv = dv + dot_tn(probs.astype(BF), d_att)
        d_probs = dot_nt(d_att, values)
        inner = jnp.sum(probs * d_probs, axis=-1, keepdims=True)
        d_scores = (probs * (d_probs - inner) * 0.0625).astype(BF)
        dk = dk + dot_tn(d_scores, q)
        dq_ref[h] = dot(d_scores, keys)
    dkv_ref[:, :256] = dk
    dkv_ref[:, 256:] = dv


def project_back_kernel(
    core_ref, x0, x1, x2, normed_ref, qraw_ref, kraw_ref, own, oth, cos_ref, sin_ref, gain_ref, dgain_ref, c5, c2,
    dq_ref, dkv_ref, dhid_ref, dx0, dx1, dx2, g_own, g_oth,
):
    first = core_ref[0] == 0
    c, s = (cos_ref[...], sin_ref[...])
    gain_q, gain_k = (gain_ref[4:5, :256], gain_ref[5:6, :256])
    dk, dv = (dkv_ref[:, :256], dkv_ref[:, 256:])
    d_gain_q = 0.0
    d_qs = []
    for h in range(4):
        d, dg = rms_back(qraw_ref[h], gain_q, turn_back(dq_ref[h], c[512:], s[512:]))
        d_gain_q = d_gain_q + dg
        d_qs.append(d.astype(BF))
    d_k, d_gain_k = rms_back(kraw_ref[...], gain_k, turn_back(dk, c, s))
    left = jnp.concatenate([d_k[:, :128], dv[:, :128]], axis=1)
    right = jnp.concatenate([d_k[:, 128:], dv[:, 128:]], axis=1)
    sides = (jnp.where(first, left, right).astype(BF), jnp.where(first, right, left).astype(BF))
    d_query = d_normed = 0.0
    for side, (w, ref) in enumerate(((own, g_own), (oth, g_oth))):
        d_q = jnp.concatenate(d_qs[2 * side : 2 * side + 2], axis=1)
        put_panels(ref, 0, dot_tn(normed_ref[512:, :], d_q), ROWS)
        put_panels(ref, 4 * ROWS, dot_tn(normed_ref[...], sides[side]), ROWS)
        d_query = d_query + dot_nt(d_q, columns(w, 0, 4))
        d_normed = d_normed + dot_nt(sides[side], columns(w, 4, 2))
    d_in = 0.0
    for n, (x_ref, out) in enumerate(((x2, dx2), (x1, dx1), (x0, dx0))):
        d = d_normed[n * 256 : (n + 1) * 256]
        if n == 2:
            d = d + d_query
        dx, dg = rms_back(x_ref[...].astype(F32), gain_ref[0:1, :], d)
        d_in = d_in + dg
        out[...] = (dx + dhid_ref[...] if n == 2 else dx).astype(out.dtype)
    mask5, mask2 = (owner_mask(640, 5), owner_mask(256, 2))
    lane5 = lax.broadcasted_iota(jnp.int32, (640, 128), 1)
    lane2 = lax.broadcasted_iota(jnp.int32, (256, 128), 1)
    table = 0.0
    for n, d in enumerate((d_in, dgain_ref[0:1, :], dgain_ref[1:2, :], dgain_ref[2:3, :])):
        place = (lane5 == c5[...] + 5 * n).astype(F32).astype(BF)
        table = table + dot(jnp.where(mask5, d, 0.0).astype(BF), place)
    for n, d in enumerate((d_gain_q, d_gain_k)):
        place = (lane2 == c2[...] + 20 + 2 * n).astype(F32).astype(BF)
        table = table + dot(jnp.where(mask2, d, 0.0).astype(BF), place)
    feature = lax.broadcasted_iota(jnp.int32, (640, 128), 0)
    owner = lax.broadcasted_iota(jnp.int32, (640, 128), 1)
    table = dot((feature == 5 * owner).astype(F32).astype(BF), table.astype(BF))
    for ref in (g_own, g_oth):
        put_panels(ref, 6 * ROWS, table, ROWS)


def call(kernel, outs, args, scratch=(), name=None):
    vmem = pl.BlockSpec(memory_space=pltpu.VMEM)
    smem = pl.BlockSpec(memory_space=pltpu.SMEM)
    return pl.pallas_call(
        kernel,
        out_shape=[jax.ShapeDtypeStruct(shape, dtype) for shape, dtype in outs],
        in_specs=[smem if a.shape == (1,) else vmem for a in args],
        out_specs=[vmem] * len(outs),
        scratch_shapes=list(scratch),
        compiler_params=pltpu.CompilerParams(vmem_limit_bytes=60 * 1024 * 1024),
        name=name,
    )(*args)


def halves(a):
    rows, width = a.shape
    if width % 256:
        cut = a.reshape(rows, -1, 128).transpose(1, 0, 2)
        part = (width + 128) // 256
        return jnp.stack([cut[:part], cut[-part:]]).reshape(2, -1, 128)
    return a.reshape(rows, 2, -1, 128).transpose(1, 2, 0, 3).reshape(2, -1, 128)


def to_all(flat, before, after):
    wide = jnp.broadcast_to(flat[None, :, None], (before, 2, after, *flat.shape[1:]))
    return wide.reshape(-1, *flat.shape[1:])


def block_of(near, at, panel_count, rows):
    cut = near[:, at : at + panel_count * rows].reshape(-1, panel_count, rows, 128)
    return cut.transpose(1, 0, 2, 3).reshape(-1, 128)


def pieces_of(block, panel_count, rows):
    cut = block.reshape(panel_count, -1, rows, 128)
    return cut.transpose(1, 0, 2, 3).reshape(cut.shape[1], -1, 128)


def whole(cut, panel_count, rows, width):
    cut = cut.reshape(2, panel_count, rows, 128)
    if width % 256:
        cut = jnp.concatenate([cut[0, : width // 128 - panel_count], cut[1]], axis=0)
        return cut.transpose(1, 0, 2).reshape(rows, width)
    return cut.transpose(2, 0, 1, 3).reshape(rows, width)


def body(
    tokens, positions, w_query, w_key, w_value, w_out, w_gate, w_up, w_down,
    norm_input, norm_post_attn, norm_pre_ff, norm_post_ff, norm_query, norm_key, cotangent,
):
    core = lax.axis_index("core").astype(jnp.int32).reshape(1)
    x = tokens.reshape(256, 640)
    g = cotangent.reshape(256, 640)

    def along(v, distance):
        return lax.ppermute(v, SEQ, [(i - distance, i) for i in range(8) if 0 <= i - distance < 8])

    x1, x2 = (along(x, 1), along(x, 2))
    place = positions.reshape(256, 1)
    before = positions[:, :1] - jnp.arange(512, 0, -1, dtype=jnp.int32)[None]
    places = jnp.concatenate([before, positions], axis=1).reshape(768, 1)
    steps = jnp.arange(128).astype(F32)
    angles = places.astype(F32) * (10000.0 ** (-2.0 * steps / 256))
    cos, sin = (jnp.cos(angles), jnp.sin(angles))
    m5, m2 = [jnp.asarray((np.arange(n) % k).astype(np.int32)) for n, k in ((640, 5), (256, 2))]

    gain_row = jnp.concatenate([norm_input, norm_post_attn, norm_pre_ff, norm_post_ff, norm_query, norm_key])
    gain_row = jnp.pad(gain_row, (0, 104)).reshape(1, 1, 128)
    flat = jnp.concatenate(
        [halves(w_query), halves(w_key), halves(w_value), jnp.broadcast_to(gain_row, (2, 1, 128))], axis=1
    )
    flat_ff = jnp.concatenate([halves(w_out), halves(w_gate), halves(w_up)], axis=1)
    near = lax.all_to_all(to_all(flat_ff, 2, 8), NEAR_Z, 0, 0)
    flat = jnp.concatenate([halves(w_down), flat], axis=1)
    near, flat, cos, sin, place = lax.optimization_barrier((near, flat, cos, sin, place))
    block = jnp.concatenate([block_of(near, 0, 3, 8), block_of(near, 24, 8, 5), block_of(near, 64, 8, 5)])
    f_own = lax.all_gather(block, "z")

    near = lax.all_to_all(to_all(flat, 8, 8), AXES, 0, 0)
    q_own = jnp.concatenate(
        [block_of(near, 48, 4, 5), block_of(near, 68, 1, 5), block_of(near, 73, 1, 5), near[:, 78]]
    )
    q_own, x1, x2 = lax.optimization_barrier((q_own, x1, x2))
    q_oth = lax.ppermute(q_own, "core", SWAP)
    d_own = near[:, :48]
    d_oth = lax.ppermute(d_own, "core", SWAP)
    normed, q_raw, k_raw, q, kv, gains, attended, log_total = call(
        attend_kernel,
        [((768, 640), BF), ((4, 256, 256), F32), ((768, 256), F32), ((4, 256, 256), BF), ((768, 512), BF), ((8, 640), F32),
         ((4, 256, 256), BF), ((4, 256, 128), F32)],
        (core, x, x1, x2, q_own, q_oth, cos, sin, place, m5.reshape(1, 640), m2.reshape(1, 256)),
        name="attend",
    )
    f_own, attended = lax.optimization_barrier((f_own, attended))
    f_oth = lax.ppermute(f_own, "core", SWAP)
    mixed, d_hidden, d_att, d_gains, gff_own, gff_oth, gx_own, gx_oth = call(
        feed_kernel,
        [((256, 640), BF), ((256, 640), F32), ((4, 256, 256), BF), ((8, 640), F32)]
        + [((4, 2560, 128), BF)] * 2 + [((128, 80, 128), BF)] * 2,
        (core, x, g, attended, gains, f_own, f_oth, d_own, d_oth),
        name="feed",
    )

    def both(mine, theirs):
        return (mine.astype(F32) + lax.ppermute(theirs.astype(BF), "core", SWAP).astype(F32)).astype(BF)

    gff, gx = (both(gff_own, gff_oth), both(gx_own, gx_oth)[:, :72])
    gx = gx.reshape(4, 2, 2, 2, 4, 72, 128).transpose(1, 3, 0, 2, 4, 5, 6).reshape(4, 32, 72, 128)

    d_q, dkv = call(
        attend_back_kernel,
        [((4, 256, 256), F32), ((768, 512), F32)],
        (q, kv, place, log_total, d_att),
        name="attend_back",
    )
    d_q, dkv, gff, gx = lax.optimization_barrier((d_q, dkv, gff, gx))
    dx0, dx1, dx2, gq_own, gq_oth = call(
        project_back_kernel,
        [((256, 640), F32), ((256, 640), BF), ((256, 640), BF)] + [((4, 1120, 128), BF)] * 2,
        (core, x, x1, x2, normed, q_raw, k_raw, q_own, q_oth, cos, sin, gains, d_gains, m5.reshape(640, 1),
         m2.reshape(256, 1), d_q, dkv, d_hidden),
        name="project_back",
    )
    gq_got = lax.ppermute(gq_oth, "core", SWAP)
    gff_near = lax.psum_scatter(gff, "z")
    gx = lax.all_to_all(gx, Y, 0, 0)
    gq_got, gx, dx1, dx2, gff_near = lax.optimization_barrier((gq_got, gx, dx1, dx2, gff_near))
    gq = (gq_own.astype(F32) + gq_got.astype(F32)).astype(BF)

    def total(back, before, after):
        return back.reshape(before, 2, after, *back.shape[1:]).astype(F32).sum((0, 2))

    gq_near = lax.psum_scatter(gq, "z")
    gx = lax.all_to_all(gx.astype(F32).sum(0).astype(BF), NEAR_Y, 0, 0)
    dx1, dx2 = (along(dx1, -1), along(dx2, -2))
    gx, dx1, dx2, gq_near = lax.optimization_barrier((gx, dx1, dx2, gq_near))
    rest = pieces_of(jnp.concatenate([gff_near, gq_near]), 23, 5)
    rest = lax.all_to_all(rest, NEAR_Z, 0, 0)
    d_x = (dx0 + dx1.astype(F32) + dx2.astype(F32)).astype(BF)
    rest, gx = (total(rest, 2, 8), total(gx, 4, 4))
    grads = [
        whole(rest[:, 80:100], 4, 5, 1024),
        whole(rest[:, 100:105], 1, 5, 256),
        whole(rest[:, 105:110], 1, 5, 256),
        whole(gx[:, 48:72], 3, 8, 640),
        whole(rest[:, :40], 8, 5, 2048),
        whole(rest[:, 40:80], 8, 5, 2048),
        whole(gx[:, :48], 3, 16, 640),
    ]
    at = 0
    for n in GAINS:
        grads.append(rest[0, 110, at : at + n])
        at += n
    return (mixed.reshape(1, 256, 640), d_x.reshape(1, 256, 640), *grads)


def solution(mesh):
    fine = Mesh(mesh.devices.reshape([size for _, size in SIZES]), AXES)
    rows, lines, wide, flat = (P(DP, SEQ, None), P(DP, SEQ), P(AXES, None), P(AXES))
    return jax.shard_map(
        body,
        mesh=fine,
        in_specs=(rows, lines) + (wide,) * 7 + (flat,) * 6 + (rows,),
        out_specs=(rows, rows) + (wide,) * 7 + (flat,) * 6,
        check_vma=False,
    )
```

profile of v0, /device:TPU:1, one launch (start us, length us, event | category | flops | bytes accessed | tf_op | source)
XLA Modules:
  0.0 253.0 jit_solution(6285924465782168245)
XLA Ops:
  7.3 0.8 slice_bitcast_fusion.6
  8.1 0.8 copy.208
  8.9 0.8 copy.207
  9.8 1.0 broadcast_in_dim.6
  10.8 8.6 %all-to-all-start = ((bf16[32,104,128]{2,1,0:T(8,128)(2,1)}), bf16[32,104,128]{2,1,0:T(8,128)(2,1)S(1)}, u32[]{:S(2)}, u32[]{:S(2)}) async-start(bf16[32,104,128]{2,1,0:T(8,128)(2,1)} %bitcast.12), calls=%async_computation | async-start | bytes 1703936 | tf_op jit(solution)/shard_map/all_to_all | solution.py:389
  19.5 0.5 slice.101
  20.5 0.7 add_subtract_fusion
  21.2 2.5 multiply_sine_fusion
  23.7 10.7 %all-to-all-done = bf16[32,104,128]{2,1,0:T(8,128)(2,1)S(1)} async-done(((bf16[32,104,128]{2,1,0:T(8,128)(2,1)}), bf16[32,104,128]{2,1,0:T(8,128)(2,1)S(1)}, u32[]{:S(2)}, u32[]{:S(2)}) %all-to-all-start) | async-done | bytes 852000 | tf_op jit(solution)/shard_map/all_to_all | solution.py:389
  35.3 0.9 pad_maximum_fusion.2
  36.3 2.0 broadcast_in_dim.8
  38.3 6.7 %all-to-all-start.1 = ((bf16[128,79,128]{2,1,0:T(8,128)(2,1)}), bf16[128,79,128]{2,1,0:T(8,128)(2,1)S(1)}, u32[]{:S(2)}, u32[]{:S(2)}) async-start(bf16[128,79,128]{2,1,0:T(8,128)(2,1)} %bitcast.164), calls=%async_computation.1 | async-start | bytes 5242880 | tf_op jit(solution)/shard_map/all_to_all | solution.py:395
  45.1 4.8 %collective-permute-start.1 = (bf16[256,640]{1,0:T(8,128)(2,1)S(1)}, bf16[256,640]{1,0:T(8,128)(2,1)S(1)}, u32[]{:S(2)}, u32[]{:S(2)}) collective-permute-start(bf16[256,640]{1,0:T(8,128)(2,1)S(1)} %bitcast.175), channel_id=1, source_target_pairs={{0,2},{1,3},{2,4},{3,5},{4,6},{5,7},{8,10},{9,11},{10,12},{11,13},... | collective-permute-start | bytes 983048 | tf_op jit(solution)/shard_map/ppermute | solution.py:372
  49.9 2.9 %collective-permute-start = (bf16[256,640]{1,0:T(8,128)(2,1)S(1)}, bf16[256,640]{1,0:T(8,128)(2,1)}, u32[]{:S(2)}, u32[]{:S(2)}) collective-permute-start(bf16[256,640]{1,0:T(8,128)(2,1)S(1)} %bitcast.176), channel_id=1, source_target_pairs={{0,1},{1,2},{2,3},{3,4},{4,5},{5,6},{6,7},{8,9},{9,10},{10,11},{11... | collective-permute-start | bytes 983048 | tf_op jit(solution)/shard_map/ppermute | solution.py:372
  52.8 28.3 %all-to-all-done.1 = bf16[128,79,128]{2,1,0:T(8,128)(2,1)S(1)} async-done(((bf16[128,79,128]{2,1,0:T(8,128)(2,1)}), bf16[128,79,128]{2,1,0:T(8,128)(2,1)S(1)}, u32[]{:S(2)}, u32[]{:S(2)}) %all-to-all-start.1) | async-done | bytes 2588704 | tf_op jit(solution)/shard_map/all_to_all | solution.py:395
  81.2 0.6 copy.206
  81.8 0.9 fusion.2
  82.7 1.7 reshape_transpose_reshape.6
  84.4 0.7 reshape_transpose_reshape.7
  85.3 1.5 copy.159
  86.8 2.2 reshape.262
  89.0 2.3 pad_maximum_fusion.own
  91.2 5.7 %collective-permute-start.2 = (bf16[3968,128]{1,0:T(8,128)(2,1)}, bf16[3968,128]{1,0:T(8,128)(2,1)}, u32[]{:S(2)}, u32[]{:S(2)}) collective-permute-start(bf16[3968,128]{1,0:T(8,128)(2,1)} %pad_maximum_fusion.own), channel_id=1, source_target_pairs={{0,8},{8,0},{1,9},{9,1},{2,10},{10,2},{3,11},{11,3},{4,12},{12,4},... | collective-permute-start | bytes 3047432 | tf_op jit(solution)/shard_map/ppermute | solution.py:400
  96.9 0.8 copy.161.pos_ref
  97.7 1.8 collective-permute-done.2.oth
  99.5 7.2 %attend.1 = (bf16[768,640]{1,0:T(8,128)(2,1)}, f32[4,256,256]{2,1,0:T(8,128)}, f32[768,256]{1,0:T(8,128)}, bf16[4,256,256]{2,1,0:T(8,128)(2,1)}, bf16[768,512]{1...) custom-call(s32[1]{0:T(128)} %bitcast.core_ref, ...), custom_call_target="tpu_custom_call" | custom-call | tf_op jit(solution)/shard_map/attend/pallas_call | solution.py:320
  106.7 0.5 collective-permute-start.3
  107.2 1.1 copy-done
  108.5 6.5 %collective-permute-done.4.down_oth = bf16[128,48,128]{2,1,0:T(8,128)(2,1)S(1)} collective-permute-done((bf16[128,48,128]{2,1,0:T(8,128)(2,1)S(1)}, bf16[128,48,128]{2,1,0:T(8,128)(2,1)S(1)}, u32[]{:S(2)}, u32[]{:S(2)}) %collective-permute-start.4) | collective-permute-done | bytes 1572896 | tf_op jit(solution)/shard_map/ppermute | solution.py:402
  115.0 1.2 copy-done.3
  116.2 19.0 %feed.1 = (bf16[256,640]{1,0:T(8,128)(2,1)}, f32[256,640]{1,0:T(8,128)}, bf16[4,256,256]{2,1,0:T(8,128)(2,1)}, f32[8,640]{1,0:T(8,128)}, bf16[4,2560,128]{2,1,0:...) custom-call(s32[1]{0:T(128)} %bitcast.core_ref, ...), custom_call_target="tpu_custom_call" | custom-call | tf_op jit(solution)/shard_map/feed/pallas_call | solution.py:320
  135.9 6.3 %attend_back.1 = (f32[4,256,256]{2,1,0:T(8,128)}, f32[768,512]{1,0:T(8,128)}) custom-call(bf16[4,256,256]{2,1,0:T(8,128)(2,1)} %get-tuple-element.78.q_ref, bf16[768,512]{1,0:T(8,128)(2,1)} %get-tuple-element.79.kv_ref, s32[256,1]{1,0:T(8,128)} %copy.161.pos_ref, f32[4,256,128]{2,1,0:T(8,128)} %get-tuple-element.80.log_ref, ...), custom_call_target="tpu_custom_call" | custom-call | tf_op jit(solution)/shard_map/attend_back/pallas_call | solution.py:320
  142.2 3.0 %add_convert_fusion.1 = bf16[128,72,128]{2,1,0:T(8,128)(2,1)S(1)} fusion(bf16[128,80,128]{2,1,0:T(8,128)(2,1)} %collective-permute-done.6, bf16[128,80,128]{2,1,0:T(8,128)(2,1)} %get-tuple-element.86), kind=kLoop, calls=%fused_computation.1 | loop fusion | flops 4718592 | bytes 7077888 | tf_op jit(solution)/shard_map/convert_element_type | solution.py:421
  145.2 1.8 copy.163
  147.0 0.8 copy-done.2
  147.8 2.2 add_convert_fusion
  150.0 4.1 %all-to-all-start.2 = ((bf16[4,32,72,128]{3,2,1,0:T(8,128)(2,1)}), bf16[4,32,72,128]{3,2,1,0:T(8,128)(2,1)S(1)}, u32[]{:S(2)}, u32[]{:S(2)}) async-start(bf16[4,32,72,128]{3,2,1,0:T(8,128)(2,1)} %bitcast.166), calls=%async_computation.2 | async-start | bytes 4718592 | tf_op jit(solution)/shard_map/all_to_all | solution.py:442
  154.1 10.2 %project_back.1 = (f32[256,640]{1,0:T(8,128)}, bf16[256,640]{1,0:T(8,128)(2,1)}, bf16[256,640]{1,0:T(8,128)(2,1)}, bf16[4,1120,128]{2,1,0:T(8,128)(2,1)}, bf16[4,1120,128]{2,1,0:T(8,128)(2,1)}) custom-call(s32[1]{0:T(128)} %bitcast.core_ref, bf16[256,640]{1,0:T(8,128)(2,1)} %bitcast.174, bf16[256,640]{1,0:T(8,128)(2,1)} %collective-permute-done.x1, ...), custom_call_target="tpu_custom_call" | custom-call | tf_op jit(solution)/shard_map/project_back/pallas_call | solution.py:320
  164.3 0.5 collective-permute-start.7
  164.8 2.6 %collective-permute-done.7 = bf16[4,1120,128]{2,1,0:T(8,128)(2,1)S(1)} collective-permute-done((bf16[4,1120,128]{2,1,0:T(8,128)(2,1)}, bf16[4,1120,128]{2,1,0:T(8,128)(2,1)S(1)}, u32[]{:S(2)}, u32[]{:S(2)}) %collective-permute-start.7) | collective-permute-done | bytes 1146912 | tf_op jit(solution)/shard_map/ppermute | solution.py:440
  167.4 15.5 %all-to-all-done.2 = bf16[4,32,72,128]{3,2,1,0:T(8,128)(2,1)S(1)} async-done(((bf16[4,32,72,128]{3,2,1,0:T(8,128)(2,1)}), bf16[4,32,72,128]{3,2,1,0:T(8,128)(2,1)S(1)}, u32[]{:S(2)}, u32[]{:S(2)}) %all-to-all-start.2) | async-done | bytes 2359328 | tf_op jit(solution)/shard_map/all_to_all | solution.py:442
  182.9 2.6 %add_convert_fusion.2 = bf16[4,1120,128]{2,1,0:T(8,128)(2,1)} fusion(bf16[4,1120,128]{2,1,0:T(8,128)(2,1)S(1)} %collective-permute-done.7, bf16[4,1120,128]{2,1,0:T(8,128)(2,1)} %get-tuple-element.100), kind=kLoop, calls=%fused_computation.2 | loop fusion | flops 2293760 | bytes 3440640 | tf_op jit(solution)/shard_map/convert_element_type | solution.py:444
  185.5 1.3 reduce_sum.30
  186.8 4.9 %all-to-all-start.3 = ((bf16[32,72,128]{2,1,0:T(8,128)(2,1)}), bf16[32,72,128]{2,1,0:T(8,128)(2,1)S(1)}, u32[]{:S(2)}, u32[]{:S(2)}) async-start(bf16[32,72,128]{2,1,0:T(8,128)(2,1)} %reduce_sum.30), calls=%async_computation.4 | async-start | bytes 1179648 | tf_op jit(solution)/shard_map/all_to_all | solution.py:450
  191.7 1.3 collective-permute-start.8
  193.0 1.3 collective-permute-start.9
  194.3 13.1 %collective-permute-done.8 = bf16[256,640]{1,0:T(8,128)(2,1)S(1)} collective-permute-done((bf16[256,640]{1,0:T(8,128)(2,1)}, bf16[256,640]{1,0:T(8,128)(2,1)S(1)}, u32[]{:S(2)}, u32[]{:S(2)}) %collective-permute-start.8) | collective-permute-done | bytes 327712 | tf_op jit(solution)/shard_map/ppermute | solution.py:372
  207.4 1.4 collective-permute-done.9
  208.8 3.6 %reduce-scatter.5.cloned.1.call-done = bf16[1,1120,128]{2,1,0:T(8,128)(2,1)} async-done(((bf16[4,1120,128]{2,1,0:T(8,128)(2,1)}), bf16[1,1120,128]{2,1,0:T(8,128)(2,1)}) %reduce-scatter.5.cloned.1.call-update) | async-done | bytes 286736 | tf_op jit(solution)/shard_map/reduce_scatter | solution.py:449
  212.6 0.6 slice_bitcast_fusion.1
  213.2 1.0 pad_maximum_fusion.1
  214.8 1.4 copy.165
  216.2 9.7 %all-to-all-start.4 = ((bf16[32,115,128]{2,1,0:T(8,128)(2,1)}), bf16[32,115,128]{2,1,0:T(8,128)(2,1)S(1)}, u32[]{:S(2)}, u32[]{:S(2)}) async-start(bf16[32,115,128]{2,1,0:T(8,128)(2,1)} %copy.165), calls=%async_computation.6 | async-start | bytes 1966080 | tf_op jit(solution)/shard_map/all_to_all | solution.py:454
  225.9 0.7 slice_bitcast_fusion.4
  226.6 0.6 maximum_bitcast_fusion.1
  227.2 0.6 copy_bitcast_fusion.2
  227.8 0.8 fusion
  228.6 13.8 %all-to-all-done.4 = bf16[32,115,128]{2,1,0:T(8,128)(2,1)S(1)} async-done(((bf16[32,115,128]{2,1,0:T(8,128)(2,1)}), bf16[32,115,128]{2,1,0:T(8,128)(2,1)S(1)}, u32[]{:S(2)}, u32[]{:S(2)}) %all-to-all-start.4) | async-done | bytes 942112 | tf_op jit(solution)/shard_map/all_to_all | solution.py:454
  242.6 0.6 slice_bitcast_fusion.7
  243.2 0.6 slice_bitcast_fusion.9
  243.8 0.6 copy.209
  244.4 0.6 copy.210
  245.1 0.6 reshape.274
  245.8 0.7 copy_bitcast_fusion
  (112 shorter events, 3.7 us)
Async XLA Ops:
  7.2 12.3 %copy-start.14 = (s32[1,256]{1,0:T(1,128)S(1)}, s32[1,256]{1,0:T(1,128)}, u32[]{:S(2)}) copy-start(s32[1,256]{1,0:T(1,128)} %param.19) | copy-start | bytes 3076
  7.2 12.8 %copy-start.13 = (bf16[5,1024]{1,0:T(8,128)(2,1)S(1)}, bf16[5,1024]{1,0:T(8,128)(2,1)}, u32[]{:S(2)}) copy-start(bf16[5,1024]{1,0:T(8,128)(2,1)} %param.20) | copy-start | bytes 30724
  7.2 12.8 %copy-start.12 = (bf16[16,640]{1,0:T(8,128)(2,1)S(1)}, bf16[16,640]{1,0:T(8,128)(2,1)}, u32[]{:S(2)}) copy-start(bf16[16,640]{1,0:T(8,128)(2,1)} %param.26) | copy-start | bytes 61444
  7.2 12.9 %copy-start.22 = (bf16[2]{0:T(256)(128)(2,1)S(1)}, bf16[2]{0:T(256)(128)(2,1)}, u32[]{:S(2)}) copy-start(bf16[2]{0:T(256)(128)(2,1)} %param.32) | copy-start | bytes 16
  7.2 12.9 %copy-start.21 = (bf16[2]{0:T(256)(128)(2,1)S(1)}, bf16[2]{0:T(256)(128)(2,1)}, u32[]{:S(2)}) copy-start(bf16[2]{0:T(256)(128)(2,1)} %param.31) | copy-start | bytes 16
  7.2 12.9 %copy-start.20 = (bf16[5]{0:T(256)(128)(2,1)S(1)}, bf16[5]{0:T(256)(128)(2,1)}, u32[]{:S(2)}) copy-start(bf16[5]{0:T(256)(128)(2,1)} %param.30) | copy-start | bytes 34
  7.2 12.9 %copy-start.19 = (bf16[5]{0:T(256)(128)(2,1)S(1)}, bf16[5]{0:T(256)(128)(2,1)}, u32[]{:S(2)}) copy-start(bf16[5]{0:T(256)(128)(2,1)} %param.29) | copy-start | bytes 34
  7.3 12.9 %copy-start.18 = (bf16[5]{0:T(256)(128)(2,1)S(1)}, bf16[5]{0:T(256)(128)(2,1)}, u32[]{:S(2)}) copy-start(bf16[5]{0:T(256)(128)(2,1)} %param.28) | copy-start | bytes 34
  7.3 12.9 %copy-start.17 = (bf16[5]{0:T(256)(128)(2,1)S(1)}, bf16[5]{0:T(256)(128)(2,1)}, u32[]{:S(2)}) copy-start(bf16[5]{0:T(256)(128)(2,1)} %param.27) | copy-start | bytes 34
  7.3 13.1 %copy-start.16 = (bf16[5,256]{1,0:T(8,128)(2,1)S(1)}, bf16[5,256]{1,0:T(8,128)(2,1)}, u32[]{:S(2)}) copy-start(bf16[5,256]{1,0:T(8,128)(2,1)} %param.22) | copy-start | bytes 7684
  7.3 13.1 %copy-start.15 = (bf16[5,256]{1,0:T(8,128)(2,1)S(1)}, bf16[5,256]{1,0:T(8,128)(2,1)}, u32[]{:S(2)}) copy-start(bf16[5,256]{1,0:T(8,128)(2,1)} %param.21) | copy-start | bytes 7684
  10.8 23.6 %all-to-all-start = ((bf16[32,104,128]{2,1,0:T(8,128)(2,1)}), bf16[32,104,128]{2,1,0:T(8,128)(2,1)S(1)}, u32[]{:S(2)}, u32[]{:S(2)}) async-start(bf16[32,104,128]{2,1,0:T(8,128)(2,1)} %bitcast.12), calls=%async_computation | async-start | bytes 1703936 | tf_op jit(solution)/shard_map/all_to_all | solution.py:389
  19.4 87.3 %all-gather.3.cloned.1.call-start = ((), (), s32[]{:S(2)}) async-start(), calls=%async_computation.9 | async-start | bytes 4259840 | tf_op jit(solution)/shard_map/all_gather | solution.py:393
  38.3 6.8 %copy-start.1 = (bf16[1,256,640]{2,1,0:T(8,128)(2,1)S(1)}, bf16[1,256,640]{2,1,0:T(8,128)(2,1)}, u32[]{:S(2)}) copy-start(bf16[1,256,640]{2,1,0:T(8,128)(2,1)} %param.18) | copy-start | bytes 983044
  38.3 42.8 %all-to-all-start.1 = ((bf16[128,79,128]{2,1,0:T(8,128)(2,1)}), bf16[128,79,128]{2,1,0:T(8,128)(2,1)S(1)}, u32[]{:S(2)}, u32[]{:S(2)}) async-start(bf16[128,79,128]{2,1,0:T(8,128)(2,1)} %bitcast.164), calls=%async_computation.1 | async-start | bytes 5242880 | tf_op jit(solution)/shard_map/all_to_all | solution.py:395
  45.0 137.8 %reduce-scatter.3.cloned.1.call-start = ((), (), s32[]{:S(2)}) async-start(), calls=%async_computation.7 | async-start | bytes 3276800 | tf_op jit(solution)/shard_map/reduce_scatter | solution.py:441
  45.1 46.1 %collective-permute-start.1 = (bf16[256,640]{1,0:T(8,128)(2,1)S(1)}, bf16[256,640]{1,0:T(8,128)(2,1)S(1)}, u32[]{:S(2)}, u32[]{:S(2)}) collective-permute-start(bf16[256,640]{1,0:T(8,128)(2,1)S(1)} %bitcast.175), channel_id=1, source_target_pairs={{0,2},{1,3},{2,4},{3,5},{4,6},{5,7},{8,10},{9,11},{10,12},{11,13},... | collective-permute-start | bytes 983048 | tf_op jit(solution)/shard_map/ppermute | solution.py:372
  49.9 41.3 %collective-permute-start = (bf16[256,640]{1,0:T(8,128)(2,1)S(1)}, bf16[256,640]{1,0:T(8,128)(2,1)}, u32[]{:S(2)}, u32[]{:S(2)}) collective-permute-start(bf16[256,640]{1,0:T(8,128)(2,1)S(1)} %bitcast.176), channel_id=1, source_target_pairs={{0,1},{1,2},{2,3},{3,4},{4,5},{5,6},{6,7},{8,9},{9,10},{10,11},{11... | collective-permute-start | bytes 983048 | tf_op jit(solution)/shard_map/ppermute | solution.py:372
  85.2 3.8 %copy-start.7 = (bf16[640,128]{1,0:T(8,128)(2,1)S(1)}, bf16[640,128]{1,0:T(8,128)(2,1)}, u32[]{:S(2)}) copy-start(bf16[640,128]{1,0:T(8,128)(2,1)} %reshape_transpose_reshape.6) | copy-start | bytes 491524
  85.2 3.8 %copy-start.11 = (bf16[128,1,128]{2,0,1:T(8,128)(2,1)S(1)}, bf16[128,1,128]{2,0,1:T(8,128)(2,1)}, u32[]{:S(2)}) copy-start(bf16[128,1,128]{2,0,1:T(8,128)(2,1)} %copy.206) | copy-start | bytes 98308
  91.2 8.3 %copy-start.4 = (bf16[256,640]{1,0:T(8,128)(2,1)}, bf16[256,640]{1,0:T(8,128)(2,1)S(1)}, u32[]{:S(2)}) copy-start(bf16[256,640]{1,0:T(8,128)(2,1)S(1)} %collective-permute-done.1.x2) | copy-start | bytes 983044
  91.2 8.3 %collective-permute-start.2 = (bf16[3968,128]{1,0:T(8,128)(2,1)}, bf16[3968,128]{1,0:T(8,128)(2,1)}, u32[]{:S(2)}, u32[]{:S(2)}) collective-permute-start(bf16[3968,128]{1,0:T(8,128)(2,1)} %pad_maximum_fusion.own), channel_id=1, source_target_pairs={{0,8},{8,0},{1,9},{9,1},{2,10},{10,2},{3,11},{11,3},{4,12},{12,4},... | collective-permute-start | bytes 3047432 | tf_op jit(solution)/shard_map/ppermute | solution.py:400
  106.7 8.4 %collective-permute-start.3 = (bf16[4,3328,128]{2,1,0:T(8,128)(2,1)}, bf16[4,3328,128]{2,1,0:T(8,128)(2,1)}, u32[]{:S(2)}, u32[]{:S(2)}) collective-permute-start(bf16[4,3328,128]{2,1,0:T(8,128)(2,1)} %bitcast.170), channel_id=1, source_target_pairs={{0,8},{8,0},{1,9},{9,1},{2,10},{10,2},{3,11},{11,3},{4,12},{12,4},... | collective-permute-start | bytes 10223624 | tf_op jit(solution)/shard_map/ppermute | solution.py:411
  107.2 1.1 copy-start
  108.4 6.7 %collective-permute-start.4 = (bf16[128,48,128]{2,1,0:T(8,128)(2,1)S(1)}, bf16[128,48,128]{2,1,0:T(8,128)(2,1)S(1)}, u32[]{:S(2)}, u32[]{:S(2)}) collective-permute-start(bf16[128,48,128]{2,1,0:T(8,128)(2,1)S(1)} %slice.136.down_own), channel_id=1, source_target_pairs={{0,8},{8,0},{1,9},{9,1},{2,10},{10,2},{3,11},{11,3},{4,12},{12,4},... | collective-permute-start | bytes 4718600 | tf_op jit(solution)/shard_map/ppermute | solution.py:402
  115.0 1.2 copy-start.3
  135.2 7.0 %collective-permute-start.6 = (bf16[128,80,128]{2,1,0:T(8,128)(2,1)}, bf16[128,80,128]{2,1,0:T(8,128)(2,1)}, u32[]{:S(2)}, u32[]{:S(2)}) collective-permute-start(bf16[128,80,128]{2,1,0:T(8,128)(2,1)} %get-tuple-element.87), channel_id=1, source_target_pairs={{0,8},{8,0},{1,9},{9,1},{2,10},{10,2},{3,11},{11,3},{4,12},{12,4},... | collective-permute-start | bytes 7864328 | tf_op jit(solution)/shard_map/ppermute | solution.py:421
  135.6 11.5 %collective-permute-start.5 = (bf16[4,2560,128]{2,1,0:T(8,128)(2,1)}, bf16[4,2560,128]{2,1,0:T(8,128)(2,1)S(1)}, u32[]{:S(2)}, u32[]{:S(2)}) collective-permute-start(bf16[4,2560,128]{2,1,0:T(8,128)(2,1)} %get-tuple-element.85), channel_id=1, source_target_pairs={{0,8},{8,0},{1,9},{9,1},{2,10},{10,2},{3,11},{11,3},{4,12},{12,4},... | collective-permute-start | bytes 7864328 | tf_op jit(solution)/shard_map/ppermute | solution.py:421
  145.2 2.6 %copy-start.2 = (bf16[4,2560,128]{2,1,0:T(8,128)(2,1)S(1)}, bf16[4,2560,128]{2,1,0:T(8,128)(2,1)}, u32[]{:S(2)}) copy-start(bf16[4,2560,128]{2,1,0:T(8,128)(2,1)} %get-tuple-element.84) | copy-start | bytes 7864324
  150.0 32.9 %all-to-all-start.2 = ((bf16[4,32,72,128]{3,2,1,0:T(8,128)(2,1)}), bf16[4,32,72,128]{3,2,1,0:T(8,128)(2,1)S(1)}, u32[]{:S(2)}, u32[]{:S(2)}) async-start(bf16[4,32,72,128]{3,2,1,0:T(8,128)(2,1)} %bitcast.166), calls=%async_computation.2 | async-start | bytes 4718592 | tf_op jit(solution)/shard_map/all_to_all | solution.py:442
  154.1 58.3 %reduce-scatter.5.cloned.1.call-start = ((), (), s32[]{:S(2)}) async-start(), calls=%async_computation.8 | async-start | bytes 1433600 | tf_op jit(solution)/shard_map/reduce_scatter | solution.py:449
  164.3 3.1 %collective-permute-start.7 = (bf16[4,1120,128]{2,1,0:T(8,128)(2,1)}, bf16[4,1120,128]{2,1,0:T(8,128)(2,1)S(1)}, u32[]{:S(2)}, u32[]{:S(2)}) collective-permute-start(bf16[4,1120,128]{2,1,0:T(8,128)(2,1)} %get-tuple-element.92), channel_id=1, source_target_pairs={{0,8},{8,0},{1,9},{9,1},{2,10},{10,2},{3,11},{11,3},{4,12},{12,4},... | collective-permute-start | bytes 3440648 | tf_op jit(solution)/shard_map/ppermute | solution.py:440
  185.5 27.7 %copy-start.6 = (bf16[1,2560,128]{2,1,0:T(8,128)(2,1)S(1)}, bf16[1,2560,128]{2,1,0:T(8,128)(2,1)}, u32[]{:S(2)}) copy-start(bf16[1,2560,128]{2,1,0:T(8,128)(2,1)} %reduce-scatter.3.cloned.1.call-done) | copy-start | bytes 1966084
  186.8 22.0 %all-to-all-start.3 = ((bf16[32,72,128]{2,1,0:T(8,128)(2,1)}), bf16[32,72,128]{2,1,0:T(8,128)(2,1)S(1)}, u32[]{:S(2)}, u32[]{:S(2)}) async-start(bf16[32,72,128]{2,1,0:T(8,128)(2,1)} %reduce_sum.30), calls=%async_computation.4 | async-start | bytes 1179648 | tf_op jit(solution)/shard_map/all_to_all | solution.py:450
  191.7 15.7 %collective-permute-start.8 = (bf16[256,640]{1,0:T(8,128)(2,1)}, bf16[256,640]{1,0:T(8,128)(2,1)S(1)}, u32[]{:S(2)}, u32[]{:S(2)}) collective-permute-start(bf16[256,640]{1,0:T(8,128)(2,1)} %get-tuple-element.98), channel_id=1, source_target_pairs={{1,0},{2,1},{3,2},{4,3},{5,4},{6,5},{7,6},{9,8},{10,9},{11,10},{12... | collective-permute-start | bytes 983048 | tf_op jit(solution)/shard_map/ppermute | solution.py:372
  193.0 15.8 %collective-permute-start.9 = (bf16[256,640]{1,0:T(8,128)(2,1)}, bf16[256,640]{1,0:T(8,128)(2,1)S(1)}, u32[]{:S(2)}, u32[]{:S(2)}) collective-permute-start(bf16[256,640]{1,0:T(8,128)(2,1)} %get-tuple-element.99), channel_id=1, source_target_pairs={{2,0},{3,1},{4,2},{5,3},{6,4},{7,5},{10,8},{11,9},{12,10},{13,11},... | collective-permute-start | bytes 983048 | tf_op jit(solution)/shard_map/ppermute | solution.py:372
  208.8 4.4 %copy-start.9 = (bf16[256,640]{1,0:T(8,128)(2,1)}, bf16[256,640]{1,0:T(8,128)(2,1)S(1)}, u32[]{:S(2)}) copy-start(bf16[256,640]{1,0:T(8,128)(2,1)S(1)} %collective-permute-done.9) | copy-start | bytes 983044
  212.5 2.3 copy-start.8
  214.8 13.0 %copy-start.5 = (f32[256,640]{1,0:T(8,128)S(1)}, f32[256,640]{1,0:T(8,128)}, u32[]{:S(2)}) copy-start(f32[256,640]{1,0:T(8,128)} %get-tuple-element.91) | copy-start | bytes 1966084
  214.8 13.0 %copy-start.10 = (bf16[256,640]{1,0:T(8,128)(2,1)S(1)}, bf16[256,640]{1,0:T(8,128)(2,1)}, u32[]{:S(2)}) copy-start(bf16[256,640]{1,0:T(8,128)(2,1)} %copy-done.9) | copy-start | bytes 983044
  214.8 12.4 %slice-start = ((f32[2,72,128]{2,1,0:T(8,128)}), f32[2,48,128]{2,1,0:T(8,128)S(1)}, s32[]{:S(2)}) async-start(f32[2,72,128]{2,1,0:T(8,128)} %copy-done.8), calls=%async_computation.10 | async-start | bytes 98304 | tf_op jit(solution)/shard_map/slice | solution.py:464
  216.2 26.3 %all-to-all-start.4 = ((bf16[32,115,128]{2,1,0:T(8,128)(2,1)}), bf16[32,115,128]{2,1,0:T(8,128)(2,1)S(1)}, u32[]{:S(2)}, u32[]{:S(2)}) async-start(bf16[32,115,128]{2,1,0:T(8,128)(2,1)} %copy.165), calls=%async_computation.6 | async-start | bytes 1966080 | tf_op jit(solution)/shard_map/all_to_all | solution.py:454
Sparse Core Ops, SparseCore 0:
  36.4 68.2 all-gather.2
  150.1 31.3 reduce-scatter.2
  185.6 26.7 reduce-scatter.4
where the time goes:
time: 254 us; the launch traced here: 253 us
  waiting for transfers between devices  97.4 us (38%)
  starting transfers between devices  51.8 us (20%)
  Pallas kernels  42.7 us (17%)
  local copies, waits for them, and re-layouts  27.8 us (11%)
  other arithmetic  18.9 us (7%)
  between operations  14.4 us (6%)
    pallas_call x4, Pallas kernels, call(): pl.pallas_call(kernel, out_shape=[jax.ShapeDtypeStruct(shape, dtype) for...  42.7 us
    all_to_all x1, waiting for transfers between devices, body(): near = lax.all_to_all(to_all(flat, 8, 8), AXES, 0, 0)  28.3 us
    all_to_all x1, waiting for transfers between devices, body(): gx = lax.all_to_all(gx, Y, 0, 0)  15.5 us
    ppermute x4, waiting for transfers between devices, along(): lax.ppermute(v, SEQ, [(i - distance, i) for i in range(8) if 0 <= i - dis...  14.5 us
    all_to_all x1, waiting for transfers between devices, body(): rest = lax.all_to_all(rest, NEAR_Z, 0, 0)  13.8 us
    all_to_all x1, waiting for transfers between devices, body(): near = lax.all_to_all(to_all(flat_ff, 2, 8), NEAR_Z, 0, 0)  10.7 us
    ppermute x4, starting transfers between devices, along(): lax.ppermute(v, SEQ, [(i - distance, i) for i in range(8) if 0 <= i - dis...  10.3 us
    all_to_all x1, starting transfers between devices, body(): rest = lax.all_to_all(rest, NEAR_Z, 0, 0)  9.68 us
  transfers between devices with their start and end apart: 18, of which 10 were waited for; matrix products, arithmetic and copies ran while one was open for 10% of the time, Pallas kernels for 9%

commit v1 on v0

--- a/solution.py
+++ b/solution.py
@@ -97,11 +97,11 @@
 
 
 def attend_kernel(
-    core_ref, x0, x1, x2, own, oth, cos_ref, sin_ref, pos_ref, m5, m2,
+    core_ref, x0, x1, x2, own, oth, table_ref, cos_ref, sin_ref, pos_ref, m5, m2,
     normed_ref, qraw_ref, kraw_ref, q_ref, kv_ref, gain_ref, att_ref, log_ref,
 ):
     first = core_ref[0] == 0
-    table = own[3840:3968, :]
+    table = table_ref[...]
     wide = dot_tn(table, owner_mask(640, 5).astype(BF))
     thin = dot_tn(table, owner_mask(256, 2).astype(BF))
     lane5 = lax.broadcasted_iota(jnp.int32, (128, 640), 0)
@@ -213,12 +213,13 @@
     d_in = 0.0
     for hand in range(2):
         slope, gelu, product = kept[hand]
-        begin = lax.rem(core + hand, 2) * 64
         for ref, d in ((gx_own, d_own), (gx_oth, d_oth)):
             grad = dot_tn(product, d).astype(BF)
             for p in range(3):
-                cut = grad[:, p * 128 : (p + 1) * 128].reshape(64, 16, 128)
-                ref[pl.ds(begin, 64), p * 16 : (p + 1) * 16] = cut
+                cut = grad[:, p * 128 : (p + 1) * 128].reshape(2, 2, 2, 2, 4, 16, 128)
+                for z, yh, c, yl in np.ndindex(2, 2, 2, 2):
+                    at = (2 * lax.rem(core + hand, 2) + z) * 8 + c * 4
+                    ref[2 * yh + yl, pl.ds(at, 4), p * 16 : (p + 1) * 16] = cut[z, yh, c, yl]
         d_product = dot_nt(d_own, down_rows(down_own, hand)) + dot_nt(d_oth_once, down_rows(down_oth, hand))
         d_gate, d_up = ((d_product * slope).astype(BF), (d_product * gelu).astype(BF))
         ref = (gff_own, gff_oth)[hand]
@@ -237,8 +238,11 @@
             cut = [grad[:, p * 128 : (p + 1) * 128].reshape(32, 8, 128) for p in range(3)]
             cut.append(jnp.zeros_like(cut[0]))
             for pair in range(2):
-                rows = jnp.concatenate(cut[2 * pair : 2 * pair + 2], axis=1)
-                ref[pl.ds(block * 32, 32), 48 + pair * 16 : 64 + pair * 16] = rows.astype(BF)
+                rows = jnp.concatenate(cut[2 * pair : 2 * pair + 2], axis=1).astype(BF)
+                rows = rows.reshape(2, 2, 2, 4, 16, 128)
+                for yh, c, yl in np.ndindex(2, 2, 2):
+                    at = block * 8 + c * 4
+                    ref[2 * yh + yl, pl.ds(at, 4), 48 + pair * 16 : 64 + pair * 16] = rows[yh, c, yl]
         datt_ref[s] = (dot_nt(d_own, out_own[s]) + dot_nt(d_oth_once, out_oth[s])).astype(BF)
     dgain_ref[0:1, :] = d_pa
     dgain_ref[1:2, :] = d_pf
@@ -314,6 +318,30 @@
         put_panels(ref, 6 * ROWS, table, ROWS)
 
 
+def finish_kernel(rest_ref, gx_ref, wq, wk, wv, wout, wgate, wup, wdown, *others):
+    *gains, rest, gx = others
+    for core in range(2):
+        rest[core, 112:, :] = jnp.zeros((8, 128), F32)
+        for ref, total, after in ((rest_ref, rest, 8), (gx_ref, gx, 4)):
+            acc = 0.0
+            for i in range(32):
+                if i // after % 2 == core:
+                    acc = acc + ref[i].astype(F32)
+            total[core, : acc.shape[0], :] = acc
+    for out, begin, count in ((wgate, 0, 8), (wup, 40, 8), (wq, 80, 4), (wk, 100, 1), (wv, 105, 1)):
+        for core in range(2):
+            for p in range(count):
+                at = (core * count + p) * 128
+                out[:, at : at + 128] = rest[core, begin + p * 5 : begin + p * 5 + 5, :]
+    for out, begin, rows in ((wdown, 0, 16), (wout, 48, 8)):
+        for n, (core, p) in enumerate(((0, 0), (0, 1), (1, 0), (1, 1), (1, 2))):
+            out[:, n * 128 : (n + 1) * 128] = gx[core, begin + p * rows : begin + (p + 1) * rows, :]
+    at = 0
+    for ref, n in zip(gains, GAINS):
+        ref[...] = rest[0, 110:111, at : at + n]
+        at += n
+
+
 def call(kernel, outs, args, scratch=(), name=None):
     vmem = pl.BlockSpec(memory_space=pltpu.VMEM)
     smem = pl.BlockSpec(memory_space=pltpu.SMEM)
@@ -352,14 +380,6 @@
     return cut.transpose(1, 0, 2, 3).reshape(cut.shape[1], -1, 128)
 
 
-def whole(cut, panel_count, rows, width):
-    cut = cut.reshape(2, panel_count, rows, 128)
-    if width % 256:
-        cut = jnp.concatenate([cut[0, : width // 128 - panel_count], cut[1]], axis=0)
-        return cut.transpose(1, 0, 2).reshape(rows, width)
-    return cut.transpose(2, 0, 1, 3).reshape(rows, width)
-
-
 def body(
     tokens, positions, w_query, w_key, w_value, w_out, w_gate, w_up, w_down,
     norm_input, norm_post_attn, norm_pre_ff, norm_post_ff, norm_query, norm_key, cotangent,
@@ -393,9 +413,7 @@
     f_own = lax.all_gather(block, "z")
 
     near = lax.all_to_all(to_all(flat, 8, 8), AXES, 0, 0)
-    q_own = jnp.concatenate(
-        [block_of(near, 48, 4, 5), block_of(near, 68, 1, 5), block_of(near, 73, 1, 5), near[:, 78]]
-    )
+    q_own, table = (block_of(near, 48, 6, 5), near[:, 78])
     q_own, x1, x2 = lax.optimization_barrier((q_own, x1, x2))
     q_oth = lax.ppermute(q_own, "core", SWAP)
     d_own = near[:, :48]
@@ -404,7 +422,7 @@
         attend_kernel,
         [((768, 640), BF), ((4, 256, 256), F32), ((768, 256), F32), ((4, 256, 256), BF), ((768, 512), BF), ((8, 640), F32),
          ((4, 256, 256), BF), ((4, 256, 128), F32)],
-        (core, x, x1, x2, q_own, q_oth, cos, sin, place, m5.reshape(1, 640), m2.reshape(1, 256)),
+        (core, x, x1, x2, q_own, q_oth, table, cos, sin, place, m5.reshape(1, 640), m2.reshape(1, 256)),
         name="attend",
     )
     f_own, attended = lax.optimization_barrier((f_own, attended))
@@ -412,7 +430,7 @@
     mixed, d_hidden, d_att, d_gains, gff_own, gff_oth, gx_own, gx_oth = call(
         feed_kernel,
         [((256, 640), BF), ((256, 640), F32), ((4, 256, 256), BF), ((8, 640), F32)]
-        + [((4, 2560, 128), BF)] * 2 + [((128, 80, 128), BF)] * 2,
+        + [((4, 2560, 128), BF)] * 2 + [((4, 32, 80, 128), BF)] * 2,
         (core, x, g, attended, gains, f_own, f_oth, d_own, d_oth),
         name="feed",
     )
@@ -420,16 +438,15 @@
     def both(mine, theirs):
         return (mine.astype(F32) + lax.ppermute(theirs.astype(BF), "core", SWAP).astype(F32)).astype(BF)
 
-    gff, gx = (both(gff_own, gff_oth), both(gx_own, gx_oth)[:, :72])
-    gx = gx.reshape(4, 2, 2, 2, 4, 72, 128).transpose(1, 3, 0, 2, 4, 5, 6).reshape(4, 32, 72, 128)
-
+    gff, gx = (both(gff_own, gff_oth), both(gx_own, gx_oth)[:, :, :72])
+
+    d_att, gff, gx = lax.optimization_barrier((d_att, gff, gx))
     d_q, dkv = call(
         attend_back_kernel,
         [((4, 256, 256), F32), ((768, 512), F32)],
         (q, kv, place, log_total, d_att),
         name="attend_back",
     )
-    d_q, dkv, gff, gx = lax.optimization_barrier((d_q, dkv, gff, gx))
     dx0, dx1, dx2, gq_own, gq_oth = call(
         project_back_kernel,
         [((256, 640), F32), ((256, 640), BF), ((256, 640), BF)] + [((4, 1120, 128), BF)] * 2,
@@ -443,30 +460,22 @@
     gq_got, gx, dx1, dx2, gff_near = lax.optimization_barrier((gq_got, gx, dx1, dx2, gff_near))
     gq = (gq_own.astype(F32) + gq_got.astype(F32)).astype(BF)
 
-    def total(back, before, after):
-        return back.reshape(before, 2, after, *back.shape[1:]).astype(F32).sum((0, 2))
-
     gq_near = lax.psum_scatter(gq, "z")
     gx = lax.all_to_all(gx.astype(F32).sum(0).astype(BF), NEAR_Y, 0, 0)
     dx1, dx2 = (along(dx1, -1), along(dx2, -2))
-    gx, dx1, dx2, gq_near = lax.optimization_barrier((gx, dx1, dx2, gq_near))
-    rest = pieces_of(jnp.concatenate([gff_near, gq_near]), 23, 5)
-    rest = lax.all_to_all(rest, NEAR_Z, 0, 0)
+    ff = pieces_of(gff_near, 16, 5)
+    gx, dx1, dx2, ff, gq_near = lax.optimization_barrier((gx, dx1, dx2, ff, gq_near))
+    rest = lax.all_to_all(jnp.concatenate([ff, pieces_of(gq_near, 7, 5)], axis=1), NEAR_Z, 0, 0)
     d_x = (dx0 + dx1.astype(F32) + dx2.astype(F32)).astype(BF)
-    rest, gx = (total(rest, 2, 8), total(gx, 4, 4))
-    grads = [
-        whole(rest[:, 80:100], 4, 5, 1024),
-        whole(rest[:, 100:105], 1, 5, 256),
-        whole(rest[:, 105:110], 1, 5, 256),
-        whole(gx[:, 48:72], 3, 8, 640),
-        whole(rest[:, :40], 8, 5, 2048),
-        whole(rest[:, 40:80], 8, 5, 2048),
-        whole(gx[:, :48], 3, 16, 640),
-    ]
-    at = 0
-    for n in GAINS:
-        grads.append(rest[0, 110, at : at + n])
-        at += n
+    grads = call(
+        finish_kernel,
+        [((5, 1024), F32), ((5, 256), F32), ((5, 256), F32), ((8, 640), F32), ((5, 2048), F32), ((5, 2048), F32),
+         ((16, 640), F32)] + [((1, n), F32) for n in GAINS],
+        (rest, gx),
+        scratch=(pltpu.VMEM((2, 120, 128), F32), pltpu.VMEM((2, 72, 128), F32)),
+        name="finish",
+    )
+    grads = [g.reshape(-1) if g.shape[0] == 1 else g for g in grads]
     return (mixed.reshape(1, 256, 640), d_x.reshape(1, 256, 640), *grads)
 
 

time: 254 us -> 251 us (0.988)
  local copies, waits for them, and re-layouts: 27.8 us -> 19.4 us
  waiting for transfers between devices: 97.4 us -> 100 us
    all_to_all x1, waiting for transfers between devices: 15.5 us -> 9.31 us  [body(): gx = lax.all_to_all(gx, Y, 0, 0)]
    ppermute x2, waiting for transfers between devices: 0.01 us -> 5.22 us  [both(): lax.ppermute(theirs.astype(BF), 'core', SWAP).astype(F32)]
    reshape x4 -> x0, local copies, waits for them, and re-layouts: 3.73 us -> none  [the longest x1 1.8 us: body(): gx.reshape(4, 2, 2, 2, 4, 72, 128).transpose(1, 3, 0, 2, 4, 5, 6)]
    all_gather x1, waiting for transfers between devices: 0.01 us -> 2.6 us  [body(): f_own = lax.all_gather(block, 'z')]
    convert_element_type x2, other arithmetic: 5.17 us -> 7.74 us  [both(): (mine.astype(F32) + lax.ppermute(theirs.astype(BF), 'core', SWAP).astype(...]
    pallas_call x4 -> x5, Pallas kernels: 42.7 us -> 44.4 us  [call(): pl.pallas_call(kernel, out_shape=[jax.ShapeDtypeStruct(shape, dtype) for...]
    unnamed x56 -> x43, local copies, waits for them, and re-layouts: 6.71 us -> 5.51 us
  transfers between devices with their start and end apart: 18 -> 18, of which waited for: 10 -> 13; matrix products, arithmetic and copies ran while one was open for 10% -> 8% of each run, Pallas kernels for 9% -> 9%
where the time goes in v1:
time: 251 us; the launch traced here: 250 us
  waiting for transfers between devices  100 us (40%)
  starting transfers between devices  53.5 us (21%)
  Pallas kernels  44.4 us (18%)
  local copies, waits for them, and re-layouts  19.4 us (8%)
  other arithmetic  18.8 us (7%)
  between operations  14.3 us (6%)
    pallas_call x5, Pallas kernels, call(): pl.pallas_call(kernel, out_shape=[jax.ShapeDtypeStruct(shape, dtype) for...  44.4 us
    all_to_all x1, waiting for transfers between devices, body(): near = lax.all_to_all(to_all(flat, 8, 8), AXES, 0, 0)  28.3 us
    all_to_all x1, waiting for transfers between devices, body(): lax.all_to_all(jnp.concatenate([ff, pieces_of(gq_near, 7, 5)], axis=1), N...  14.8 us
    ppermute x4, waiting for transfers between devices, along(): lax.ppermute(v, SEQ, [(i - distance, i) for i in range(8) if 0 <= i - dis...  14.2 us
    all_to_all x1, waiting for transfers between devices, body(): near = lax.all_to_all(to_all(flat_ff, 2, 8), NEAR_Z, 0, 0)  10.7 us
    ppermute x4, starting transfers between devices, along(): lax.ppermute(v, SEQ, [(i - distance, i) for i in range(8) if 0 <= i - dis...  10.3 us
    all_to_all x1, starting transfers between devices, body(): lax.all_to_all(jnp.concatenate([ff, pieces_of(gq_near, 7, 5)], axis=1), N...  10.3 us
    all_to_all x1, waiting for transfers between devices, body(): gx = lax.all_to_all(gx, Y, 0, 0)  9.31 us
  transfers between devices with their start and end apart: 18, of which 13 were waited for; matrix products, arithmetic and copies ran while one was open for 8% of the time, Pallas kernels for 9%

profile of v1, /device:TPU:1, one launch (start us, length us, event | category | flops | bytes accessed | tf_op | source)
XLA Modules:
  0.0 250.3 jit_solution(16080739501548769770)
XLA Ops:
  7.3 0.8 slice_bitcast_fusion.2
  8.1 0.8 copy.86
  8.9 0.8 copy.85
  9.8 1.0 broadcast_in_dim.6
  10.8 8.6 %all-to-all-start = ((bf16[32,104,128]{2,1,0:T(8,128)(2,1)}), bf16[32,104,128]{2,1,0:T(8,128)(2,1)S(1)}, u32[]{:S(2)}, u32[]{:S(2)}) async-start(bf16[32,104,128]{2,1,0:T(8,128)(2,1)} %bitcast.12), calls=%async_computation | async-start | bytes 1703936 | tf_op jit(solution)/shard_map/all_to_all | solution.py:409
  19.5 0.5 slice.40
  20.3 0.1 concatenate.22
  20.5 0.7 add_subtract_fusion
  21.2 2.5 %multiply_sine_fusion = (f32[768,128]{1,0:T(8,128)}, f32[768,128]{1,0:T(8,128)}) fusion(f32[128]{0:T(128)S(1)} %multiply_power_fusion, f32[768]{0:T(1024)S(1)} %fusion.1), kind=kLoop, calls=%fused_computation.6 | loop fusion | flops 98304 | bytes 790016 | tf_op jit(solution)/shard_map/sin | solution.py:400
  23.7 10.7 %all-to-all-done = bf16[32,104,128]{2,1,0:T(8,128)(2,1)S(1)} async-done(((bf16[32,104,128]{2,1,0:T(8,128)(2,1)}), bf16[32,104,128]{2,1,0:T(8,128)(2,1)S(1)}, u32[]{:S(2)}, u32[]{:S(2)}) %all-to-all-start) | async-done | bytes 852000 | tf_op jit(solution)/shard_map/all_to_all | solution.py:409
  34.6 0.2 copy.67
  34.8 0.1 reshape.223
  35.0 0.2 copy.69
  35.2 0.1 reshape.225
  35.3 1.0 pad_maximum_fusion.1
  36.3 2.0 broadcast_in_dim.8
  38.3 6.7 %all-to-all-start.1 = ((bf16[128,79,128]{2,1,0:T(8,128)(2,1)}), bf16[128,79,128]{2,1,0:T(8,128)(2,1)S(1)}, u32[]{:S(2)}, u32[]{:S(2)}) async-start(bf16[128,79,128]{2,1,0:T(8,128)(2,1)} %bitcast.79), calls=%async_computation.1 | async-start | bytes 5242880 | tf_op jit(solution)/shard_map/all_to_all | solution.py:415
  45.1 4.8 %collective-permute-start.1 = (bf16[256,640]{1,0:T(8,128)(2,1)S(1)}, bf16[256,640]{1,0:T(8,128)(2,1)S(1)}, u32[]{:S(2)}, u32[]{:S(2)}) collective-permute-start(bf16[256,640]{1,0:T(8,128)(2,1)S(1)} %bitcast.87), channel_id=1, source_target_pairs={{0,2},{1,3},{2,4},{3,5},{4,6},{5,7},{8,10},{9,11},{10,12},{11,13},... | collective-permute-start | bytes 983048 | tf_op jit(solution)/shard_map/ppermute | solution.py:392
  49.9 2.9 %collective-permute-start = (bf16[256,640]{1,0:T(8,128)(2,1)S(1)}, bf16[256,640]{1,0:T(8,128)(2,1)}, u32[]{:S(2)}, u32[]{:S(2)}) collective-permute-start(bf16[256,640]{1,0:T(8,128)(2,1)S(1)} %bitcast.88), channel_id=1, source_target_pairs={{0,1},{1,2},{2,3},{3,4},{4,5},{5,6},{6,7},{8,9},{9,10},{10,11},{11... | collective-permute-start | bytes 983048 | tf_op jit(solution)/shard_map/ppermute | solution.py:392
  52.8 28.3 %all-to-all-done.1 = bf16[128,79,128]{2,1,0:T(8,128)(2,1)S(1)} async-done(((bf16[128,79,128]{2,1,0:T(8,128)(2,1)}), bf16[128,79,128]{2,1,0:T(8,128)(2,1)S(1)}, u32[]{:S(2)}, u32[]{:S(2)}) %all-to-all-start.1) | async-done | bytes 2588704 | tf_op jit(solution)/shard_map/all_to_all | solution.py:415
  81.2 0.4 copy.70
  81.6 1.9 copy.71
  83.4 3.2 %reshape.228.own = bf16[3840,128]{1,0:T(8,128)(2,1)} reshape(bf16[6,128,5,128]{3,2,1,0:T(8,128)(2,1)} %copy.71) | data formatting | bytes 1966080 | tf_op jit(solution)/shard_map/reshape | solution.py:375
  86.6 5.7 %collective-permute-start.2 = (bf16[3840,128]{1,0:T(8,128)(2,1)}, bf16[3840,128]{1,0:T(8,128)(2,1)}, u32[]{:S(2)}, u32[]{:S(2)}) collective-permute-start(bf16[3840,128]{1,0:T(8,128)(2,1)} %reshape.228.own), channel_id=1, source_target_pairs={{0,8},{8,0},{1,9},{9,1},{2,10},{10,2},{3,11},{11,3},{4,12},{12,4},... | collective-permute-start | bytes 2949128 | tf_op jit(solution)/shard_map/ppermute | solution.py:418
  92.3 0.8 copy.72.pos_ref
  93.2 0.6 copy.84
  93.8 1.1 collective-permute-done.2.oth
  94.9 7.2 %attend.1 = (bf16[768,640]{1,0:T(8,128)(2,1)}, f32[4,256,256]{2,1,0:T(8,128)}, f32[768,256]{1,0:T(8,128)}, bf16[4,256,256]{2,1,0:T(8,128)(2,1)}, bf16[768,512]{1...) custom-call(s32[1]{0:T(128)} %bitcast.core_ref, ...), custom_call_target="tpu_custom_call" | custom-call | tf_op jit(solution)/shard_map/attend/pallas_call | solution.py:348
  102.1 2.6 %all-gather.3.cloned.1.call-done = bf16[13312,128]{1,0:T(8,128)(2,1)} async-done(((bf16[3328,128]{1,0:T(8,128)(2,1)}), bf16[13312,128]{1,0:T(8,128)(2,1)}) %all-gather.3.cloned.1.call-update) | async-done | bytes 3407888 | tf_op jit(solution)/shard_map/all_gather | solution.py:413
  104.7 0.5 collective-permute-start.3
  105.3 1.2 copy-done
  106.5 6.6 %collective-permute-done.4.down_oth = bf16[128,48,128]{2,1,0:T(8,128)(2,1)S(1)} collective-permute-done((bf16[128,48,128]{2,1,0:T(8,128)(2,1)S(1)}, bf16[128,48,128]{2,1,0:T(8,128)(2,1)S(1)}, u32[]{:S(2)}, u32[]{:S(2)}) %collective-permute-start.4) | collective-permute-done | bytes 1572896 | tf_op jit(solution)/shard_map/ppermute | solution.py:420
  113.1 1.2 copy-done.5
  114.2 19.0 %feed.1 = (bf16[256,640]{1,0:T(8,128)(2,1)}, f32[256,640]{1,0:T(8,128)}, bf16[4,256,256]{2,1,0:T(8,128)(2,1)}, f32[8,640]{1,0:T(8,128)}, bf16[4,2560,128]{2,1,0:...) custom-call(s32[1]{0:T(128)} %bitcast.core_ref, ...), custom_call_target="tpu_custom_call" | custom-call | tf_op jit(solution)/shard_map/feed/pallas_call | solution.py:348
  133.2 0.4 collective-permute-start.5
  133.6 0.3 collective-permute-start.6
  133.9 5.2 %collective-permute-done.5 = bf16[4,2560,128]{2,1,0:T(8,128)(2,1)S(1)} collective-permute-done((bf16[4,2560,128]{2,1,0:T(8,128)(2,1)}, bf16[4,2560,128]{2,1,0:T(8,128)(2,1)S(1)}, u32[]{:S(2)}, u32[]{:S(2)}) %collective-permute-start.5) | collective-permute-done | bytes 2621472 | tf_op jit(solution)/shard_map/ppermute | solution.py:439
  139.1 4.0 %add_convert_fusion = bf16[4,2560,128]{2,1,0:T(8,128)(2,1)} fusion(bf16[4,2560,128]{2,1,0:T(8,128)(2,1)S(1)} %collective-permute-done.5, bf16[4,2560,128]{2,1,0:T(8,128)(2,1)} %get-tuple-element.95), kind=kLoop, calls=%fused_computation | loop fusion | flops 5242880 | bytes 7864320 | tf_op jit(solution)/shard_map/convert_element_type | solution.py:439
  143.2 3.7 %add_convert_fusion.1 = bf16[4,32,72,128]{3,2,1,0:T(8,128)(2,1)} fusion(bf16[4,32,80,128]{3,2,1,0:T(8,128)(2,1)} %collective-permute-done.6, bf16[4,32,80,128]{3,2,1,0:T(8,128)(2,1)S(1)} %copy-done.4), kind=kLoop, calls=%fused_computation.1 | loop fusion | flops 4718592 | bytes 7077888 | tf_op jit(solution)/shard_map/convert_element_type | solution.py:439
  146.9 4.0 %all-to-all-start.2 = ((bf16[4,32,72,128]{3,2,1,0:T(8,128)(2,1)}), bf16[4,32,72,128]{3,2,1,0:T(8,128)(2,1)S(1)}, u32[]{:S(2)}, u32[]{:S(2)}) async-start(bf16[4,32,72,128]{3,2,1,0:T(8,128)(2,1)} %add_convert_fusion.1), calls=%async_computation.2 | async-start | bytes 4718592 | tf_op jit(solution)/shard_map/all_to_all | solution.py:459
  150.9 6.4 %attend_back.1 = (f32[4,256,256]{2,1,0:T(8,128)}, f32[768,512]{1,0:T(8,128)}) custom-call(bf16[4,256,256]{2,1,0:T(8,128)(2,1)} %get-tuple-element.91.q_ref, bf16[768,512]{1,0:T(8,128)(2,1)} %get-tuple-element.92.kv_ref, s32[256,1]{1,0:T(8,128)} %copy.72.pos_ref, f32[4,256,128]{2,1,0:T(8,128)} %get-tuple-element.93.log_ref, ...), custom_call_target="tpu_custom_call" | custom-call | tf_op jit(solution)/shard_map/attend_back/pallas_call | solution.py:348
  157.3 9.6 %project_back.1 = (f32[256,640]{1,0:T(8,128)}, bf16[256,640]{1,0:T(8,128)(2,1)}, bf16[256,640]{1,0:T(8,128)(2,1)}, bf16[4,1120,128]{2,1,0:T(8,128)(2,1)}, bf16[4,1120,128]{2,1,0:T(8,128)(2,1)}) custom-call(s32[1]{0:T(128)} %bitcast.core_ref, bf16[256,640]{1,0:T(8,128)(2,1)} %bitcast.86, bf16[256,640]{1,0:T(8,128)(2,1)} %collective-permute-done.x1, ...), custom_call_target="tpu_custom_call" | custom-call | tf_op jit(solution)/shard_map/project_back/pallas_call | solution.py:348
  166.9 0.7 collective-permute-start.7
  167.5 2.6 %collective-permute-done.7 = bf16[4,1120,128]{2,1,0:T(8,128)(2,1)S(1)} collective-permute-done((bf16[4,1120,128]{2,1,0:T(8,128)(2,1)}, bf16[4,1120,128]{2,1,0:T(8,128)(2,1)S(1)}, u32[]{:S(2)}, u32[]{:S(2)}) %collective-permute-start.7) | collective-permute-done | bytes 1146912 | tf_op jit(solution)/shard_map/ppermute | solution.py:457
  170.2 9.3 %all-to-all-done.2 = bf16[4,32,72,128]{3,2,1,0:T(8,128)(2,1)S(1)} async-done(((bf16[4,32,72,128]{3,2,1,0:T(8,128)(2,1)}), bf16[4,32,72,128]{3,2,1,0:T(8,128)(2,1)S(1)}, u32[]{:S(2)}, u32[]{:S(2)}) %all-to-all-start.2) | async-done | bytes 2359328 | tf_op jit(solution)/shard_map/all_to_all | solution.py:459
  179.5 1.1 reduce-scatter.3.cloned.1.call-done
  180.6 2.6 %add_convert_fusion.2 = bf16[4,1120,128]{2,1,0:T(8,128)(2,1)} fusion(bf16[4,1120,128]{2,1,0:T(8,128)(2,1)S(1)} %collective-permute-done.7, bf16[4,1120,128]{2,1,0:T(8,128)(2,1)} %get-tuple-element.113), kind=kLoop, calls=%fused_computation.2 | loop fusion | flops 2293760 | bytes 3440640 | tf_op jit(solution)/shard_map/convert_element_type | solution.py:461
  183.2 1.3 reduce_sum.12
  184.5 5.9 %all-to-all-start.3 = ((bf16[32,72,128]{2,1,0:T(8,128)(2,1)}), bf16[32,72,128]{2,1,0:T(8,128)(2,1)S(1)}, u32[]{:S(2)}, u32[]{:S(2)}) async-start(bf16[32,72,128]{2,1,0:T(8,128)(2,1)} %reduce_sum.12), calls=%async_computation.4 | async-start | bytes 1179648 | tf_op jit(solution)/shard_map/all_to_all | solution.py:464
  190.4 1.3 collective-permute-start.8
  191.7 1.3 collective-permute-start.9
  193.0 0.2 reshape.234
  193.4 12.7 %collective-permute-done.8 = bf16[256,640]{1,0:T(8,128)(2,1)S(1)} collective-permute-done((bf16[256,640]{1,0:T(8,128)(2,1)}, bf16[256,640]{1,0:T(8,128)(2,1)S(1)}, u32[]{:S(2)}, u32[]{:S(2)}) %collective-permute-start.8) | collective-permute-done | bytes 327712 | tf_op jit(solution)/shard_map/ppermute | solution.py:392
  206.1 1.5 collective-permute-done.9
  207.6 3.5 %reduce-scatter.5.cloned.1.call-done = bf16[1,1120,128]{2,1,0:T(8,128)(2,1)} async-done(((bf16[4,1120,128]{2,1,0:T(8,128)(2,1)}), bf16[1,1120,128]{2,1,0:T(8,128)(2,1)}) %reduce-scatter.5.cloned.1.call-update) | async-done | bytes 286736 | tf_op jit(solution)/shard_map/reduce_scatter | solution.py:463
  211.1 1.1 reshape.237
  212.2 0.1 copy.77
  212.3 0.3 copy.76
  212.6 1.1 pad_maximum_fusion
  213.7 10.3 %all-to-all-start.4 = ((bf16[32,115,128]{2,1,0:T(8,128)(2,1)}), bf16[32,115,128]{2,1,0:T(8,128)(2,1)S(1)}, u32[]{:S(2)}, u32[]{:S(2)}) async-start(bf16[32,115,128]{2,1,0:T(8,128)(2,1)} %pad_maximum_fusion), calls=%async_computation.6 | async-start | bytes 1966080 | tf_op jit(solution)/shard_map/all_to_all | solution.py:468
  224.0 1.8 fusion
  225.8 14.8 %all-to-all-done.4.rest_ref = bf16[32,115,128]{2,1,0:T(8,128)(2,1)S(1)} async-done(((bf16[32,115,128]{2,1,0:T(8,128)(2,1)}), bf16[32,115,128]{2,1,0:T(8,128)(2,1)S(1)}, u32[]{:S(2)}, u32[]{:S(2)}) %all-to-all-start.4) | async-done | bytes 942112 | tf_op jit(solution)/shard_map/all_to_all | solution.py:468
  240.6 1.0 copy-done.1
  241.6 2.2 finish.1
  (78 shorter events, 1.3 us)
Async XLA Ops:
  7.2 12.3 %copy-start.11 = (s32[1,256]{1,0:T(1,128)S(1)}, s32[1,256]{1,0:T(1,128)}, u32[]{:S(2)}) copy-start(s32[1,256]{1,0:T(1,128)} %param.19) | copy-start | bytes 3076
  7.2 12.8 %copy-start.10 = (bf16[5,1024]{1,0:T(8,128)(2,1)S(1)}, bf16[5,1024]{1,0:T(8,128)(2,1)}, u32[]{:S(2)}) copy-start(bf16[5,1024]{1,0:T(8,128)(2,1)} %param.20) | copy-start | bytes 30724
  7.2 12.8 %copy-start.9 = (bf16[16,640]{1,0:T(8,128)(2,1)S(1)}, bf16[16,640]{1,0:T(8,128)(2,1)}, u32[]{:S(2)}) copy-start(bf16[16,640]{1,0:T(8,128)(2,1)} %param.26) | copy-start | bytes 61444
  7.2 12.9 %copy-start.19 = (bf16[2]{0:T(256)(128)(2,1)S(1)}, bf16[2]{0:T(256)(128)(2,1)}, u32[]{:S(2)}) copy-start(bf16[2]{0:T(256)(128)(2,1)} %param.32) | copy-start | bytes 16
  7.2 12.9 %copy-start.18 = (bf16[2]{0:T(256)(128)(2,1)S(1)}, bf16[2]{0:T(256)(128)(2,1)}, u32[]{:S(2)}) copy-start(bf16[2]{0:T(256)(128)(2,1)} %param.31) | copy-start | bytes 16
  7.2 12.9 %copy-start.17 = (bf16[5]{0:T(256)(128)(2,1)S(1)}, bf16[5]{0:T(256)(128)(2,1)}, u32[]{:S(2)}) copy-start(bf16[5]{0:T(256)(128)(2,1)} %param.30) | copy-start | bytes 34
  7.2 12.9 %copy-start.16 = (bf16[5]{0:T(256)(128)(2,1)S(1)}, bf16[5]{0:T(256)(128)(2,1)}, u32[]{:S(2)}) copy-start(bf16[5]{0:T(256)(128)(2,1)} %param.29) | copy-start | bytes 34
  7.3 12.9 %copy-start.15 = (bf16[5]{0:T(256)(128)(2,1)S(1)}, bf16[5]{0:T(256)(128)(2,1)}, u32[]{:S(2)}) copy-start(bf16[5]{0:T(256)(128)(2,1)} %param.28) | copy-start | bytes 34
  7.3 12.9 %copy-start.14 = (bf16[5]{0:T(256)(128)(2,1)S(1)}, bf16[5]{0:T(256)(128)(2,1)}, u32[]{:S(2)}) copy-start(bf16[5]{0:T(256)(128)(2,1)} %param.27) | copy-start | bytes 34
  7.3 13.0 %copy-start.13 = (bf16[5,256]{1,0:T(8,128)(2,1)S(1)}, bf16[5,256]{1,0:T(8,128)(2,1)}, u32[]{:S(2)}) copy-start(bf16[5,256]{1,0:T(8,128)(2,1)} %param.22) | copy-start | bytes 7684
  7.3 13.0 %copy-start.12 = (bf16[5,256]{1,0:T(8,128)(2,1)S(1)}, bf16[5,256]{1,0:T(8,128)(2,1)}, u32[]{:S(2)}) copy-start(bf16[5,256]{1,0:T(8,128)(2,1)} %param.21) | copy-start | bytes 7684
  10.8 23.6 %all-to-all-start = ((bf16[32,104,128]{2,1,0:T(8,128)(2,1)}), bf16[32,104,128]{2,1,0:T(8,128)(2,1)S(1)}, u32[]{:S(2)}, u32[]{:S(2)}) async-start(bf16[32,104,128]{2,1,0:T(8,128)(2,1)} %bitcast.12), calls=%async_computation | async-start | bytes 1703936 | tf_op jit(solution)/shard_map/all_to_all | solution.py:409
  19.4 85.3 %all-gather.3.cloned.1.call-start = ((), (), s32[]{:S(2)}) async-start(), calls=%async_computation.9 | async-start | bytes 4259840 | tf_op jit(solution)/shard_map/all_gather | solution.py:413
  38.3 6.8 %copy-start.2 = (bf16[1,256,640]{2,1,0:T(8,128)(2,1)S(1)}, bf16[1,256,640]{2,1,0:T(8,128)(2,1)}, u32[]{:S(2)}) copy-start(bf16[1,256,640]{2,1,0:T(8,128)(2,1)} %param.18) | copy-start | bytes 983044
  38.3 42.8 %all-to-all-start.1 = ((bf16[128,79,128]{2,1,0:T(8,128)(2,1)}), bf16[128,79,128]{2,1,0:T(8,128)(2,1)S(1)}, u32[]{:S(2)}, u32[]{:S(2)}) async-start(bf16[128,79,128]{2,1,0:T(8,128)(2,1)} %bitcast.79), calls=%async_computation.1 | async-start | bytes 5242880 | tf_op jit(solution)/shard_map/all_to_all | solution.py:415
  45.0 135.5 %reduce-scatter.3.cloned.1.call-start = ((), (), s32[]{:S(2)}) async-start(), calls=%async_computation.7 | async-start | bytes 3276800 | tf_op jit(solution)/shard_map/reduce_scatter | solution.py:458
  45.1 41.5 %collective-permute-start.1 = (bf16[256,640]{1,0:T(8,128)(2,1)S(1)}, bf16[256,640]{1,0:T(8,128)(2,1)S(1)}, u32[]{:S(2)}, u32[]{:S(2)}) collective-permute-start(bf16[256,640]{1,0:T(8,128)(2,1)S(1)} %bitcast.87), channel_id=1, source_target_pairs={{0,2},{1,3},{2,4},{3,5},{4,6},{5,7},{8,10},{9,11},{10,12},{11,13},... | collective-permute-start | bytes 983048 | tf_op jit(solution)/shard_map/ppermute | solution.py:392
  49.9 36.7 %collective-permute-start = (bf16[256,640]{1,0:T(8,128)(2,1)S(1)}, bf16[256,640]{1,0:T(8,128)(2,1)}, u32[]{:S(2)}, u32[]{:S(2)}) collective-permute-start(bf16[256,640]{1,0:T(8,128)(2,1)S(1)} %bitcast.88), channel_id=1, source_target_pairs={{0,1},{1,2},{2,3},{3,4},{4,5},{5,6},{6,7},{8,9},{9,10},{10,11},{11... | collective-permute-start | bytes 983048 | tf_op jit(solution)/shard_map/ppermute | solution.py:392
  86.6 8.2 %copy-start.6 = (bf16[256,640]{1,0:T(8,128)(2,1)}, bf16[256,640]{1,0:T(8,128)(2,1)S(1)}, u32[]{:S(2)}) copy-start(bf16[256,640]{1,0:T(8,128)(2,1)S(1)} %collective-permute-done.1.x2) | copy-start | bytes 983044
  86.6 8.2 %collective-permute-start.2 = (bf16[3840,128]{1,0:T(8,128)(2,1)}, bf16[3840,128]{1,0:T(8,128)(2,1)}, u32[]{:S(2)}, u32[]{:S(2)}) collective-permute-start(bf16[3840,128]{1,0:T(8,128)(2,1)} %reshape.228.own), channel_id=1, source_target_pairs={{0,8},{8,0},{1,9},{9,1},{2,10},{10,2},{3,11},{11,3},{4,12},{12,4},... | collective-permute-start | bytes 2949128 | tf_op jit(solution)/shard_map/ppermute | solution.py:418
  104.7 8.4 %collective-permute-start.3 = (bf16[4,3328,128]{2,1,0:T(8,128)(2,1)}, bf16[4,3328,128]{2,1,0:T(8,128)(2,1)}, u32[]{:S(2)}, u32[]{:S(2)}) collective-permute-start(bf16[4,3328,128]{2,1,0:T(8,128)(2,1)} %bitcast.82), channel_id=1, source_target_pairs={{0,8},{8,0},{1,9},{9,1},{2,10},{10,2},{3,11},{11,3},{4,12},{12,4},... | collective-permute-start | bytes 10223624 | tf_op jit(solution)/shard_map/ppermute | solution.py:429
  105.3 1.2 copy-start
  106.4 6.6 %collective-permute-start.4 = (bf16[128,48,128]{2,1,0:T(8,128)(2,1)S(1)}, bf16[128,48,128]{2,1,0:T(8,128)(2,1)S(1)}, u32[]{:S(2)}, u32[]{:S(2)}) collective-permute-start(bf16[128,48,128]{2,1,0:T(8,128)(2,1)S(1)} %slice.54.down_own), channel_id=1, source_target_pairs={{0,8},{8,0},{1,9},{9,1},{2,10},{10,2},{3,11},{11,3},{4,12},{12,4},... | collective-permute-start | bytes 4718600 | tf_op jit(solution)/shard_map/ppermute | solution.py:420
  113.1 1.2 copy-start.5
  133.2 5.9 %collective-permute-start.5 = (bf16[4,2560,128]{2,1,0:T(8,128)(2,1)}, bf16[4,2560,128]{2,1,0:T(8,128)(2,1)S(1)}, u32[]{:S(2)}, u32[]{:S(2)}) collective-permute-start(bf16[4,2560,128]{2,1,0:T(8,128)(2,1)} %get-tuple-element.96), channel_id=1, source_target_pairs={{0,8},{8,0},{1,9},{9,1},{2,10},{10,2},{3,11},{11,3},{4,12},{12,4},... | collective-permute-start | bytes 7864328 | tf_op jit(solution)/shard_map/ppermute | solution.py:439
  133.6 9.6 %collective-permute-start.6 = (bf16[4,32,80,128]{3,2,1,0:T(8,128)(2,1)}, bf16[4,32,80,128]{3,2,1,0:T(8,128)(2,1)}, u32[]{:S(2)}, u32[]{:S(2)}) collective-permute-start(bf16[4,32,80,128]{3,2,1,0:T(8,128)(2,1)} %get-tuple-element.98), channel_id=1, source_target_pairs={{0,8},{8,0},{1,9},{9,1},{2,10},{10,2},{3,11},{11,3},{4,12},{12,4},... | collective-permute-start | bytes 7864328 | tf_op jit(solution)/shard_map/ppermute | solution.py:439
  139.1 4.0 %copy-start.4 = (bf16[4,32,80,128]{3,2,1,0:T(8,128)(2,1)S(1)}, bf16[4,32,80,128]{3,2,1,0:T(8,128)(2,1)}, u32[]{:S(2)}) copy-start(bf16[4,32,80,128]{3,2,1,0:T(8,128)(2,1)} %get-tuple-element.97) | copy-start | bytes 7864324
  146.9 32.6 %all-to-all-start.2 = ((bf16[4,32,72,128]{3,2,1,0:T(8,128)(2,1)}), bf16[4,32,72,128]{3,2,1,0:T(8,128)(2,1)S(1)}, u32[]{:S(2)}, u32[]{:S(2)}) async-start(bf16[4,32,72,128]{3,2,1,0:T(8,128)(2,1)} %add_convert_fusion.1), calls=%async_computation.2 | async-start | bytes 4718592 | tf_op jit(solution)/shard_map/all_to_all | solution.py:459
  150.9 60.2 %reduce-scatter.5.cloned.1.call-start = ((), (), s32[]{:S(2)}) async-start(), calls=%async_computation.8 | async-start | bytes 1433600 | tf_op jit(solution)/shard_map/reduce_scatter | solution.py:463
  166.9 3.3 %collective-permute-start.7 = (bf16[4,1120,128]{2,1,0:T(8,128)(2,1)}, bf16[4,1120,128]{2,1,0:T(8,128)(2,1)S(1)}, u32[]{:S(2)}, u32[]{:S(2)}) collective-permute-start(bf16[4,1120,128]{2,1,0:T(8,128)(2,1)} %get-tuple-element.104), channel_id=1, source_target_pairs={{0,8},{8,0},{1,9},{9,1},{2,10},{10,2},{3,11},{11,3},{4,12},{12,4},... | collective-permute-start | bytes 3440648 | tf_op jit(solution)/shard_map/ppermute | solution.py:457
  183.1 9.9 %copy-start.8 = (bf16[1,2560,128]{2,1,0:T(8,128)(2,1)S(1)}, bf16[1,2560,128]{2,1,0:T(8,128)(2,1)}, u32[]{:S(2)}) copy-start(bf16[1,2560,128]{2,1,0:T(8,128)(2,1)} %reduce-scatter.3.cloned.1.call-done) | copy-start | bytes 1966084
  184.5 23.1 %all-to-all-start.3 = ((bf16[32,72,128]{2,1,0:T(8,128)(2,1)}), bf16[32,72,128]{2,1,0:T(8,128)(2,1)S(1)}, u32[]{:S(2)}, u32[]{:S(2)}) async-start(bf16[32,72,128]{2,1,0:T(8,128)(2,1)} %reduce_sum.12), calls=%async_computation.4 | async-start | bytes 1179648 | tf_op jit(solution)/shard_map/all_to_all | solution.py:464
  190.4 15.7 %collective-permute-start.8 = (bf16[256,640]{1,0:T(8,128)(2,1)}, bf16[256,640]{1,0:T(8,128)(2,1)S(1)}, u32[]{:S(2)}, u32[]{:S(2)}) collective-permute-start(bf16[256,640]{1,0:T(8,128)(2,1)} %get-tuple-element.110), channel_id=1, source_target_pairs={{1,0},{2,1},{3,2},{4,3},{5,4},{6,5},{7,6},{9,8},{10,9},{11,10},{12... | collective-permute-start | bytes 983048 | tf_op jit(solution)/shard_map/ppermute | solution.py:392
  191.7 15.9 %collective-permute-start.9 = (bf16[256,640]{1,0:T(8,128)(2,1)}, bf16[256,640]{1,0:T(8,128)(2,1)}, u32[]{:S(2)}, u32[]{:S(2)}) collective-permute-start(bf16[256,640]{1,0:T(8,128)(2,1)} %get-tuple-element.111), channel_id=1, source_target_pairs={{2,0},{3,1},{4,2},{5,3},{6,4},{7,5},{10,8},{11,9},{12,10},{13,11},... | collective-permute-start | bytes 983048 | tf_op jit(solution)/shard_map/ppermute | solution.py:392
  207.6 6.1 %copy-start.3 = (bf16[32,72,128]{2,1,0:T(8,128)(2,1)}, bf16[32,72,128]{2,1,0:T(8,128)(2,1)S(1)}, u32[]{:S(2)}) copy-start(bf16[32,72,128]{2,1,0:T(8,128)(2,1)S(1)} %all-to-all-done.3.gx_ref) | copy-start | bytes 1769476
  212.3 11.6 %copy-start.7 = (f32[256,640]{1,0:T(8,128)S(1)}, f32[256,640]{1,0:T(8,128)}, u32[]{:S(2)}) copy-start(f32[256,640]{1,0:T(8,128)} %get-tuple-element.103) | copy-start | bytes 1966084
  213.7 26.9 %all-to-all-start.4 = ((bf16[32,115,128]{2,1,0:T(8,128)(2,1)}), bf16[32,115,128]{2,1,0:T(8,128)(2,1)S(1)}, u32[]{:S(2)}, u32[]{:S(2)}) async-start(bf16[32,115,128]{2,1,0:T(8,128)(2,1)} %pad_maximum_fusion), calls=%async_computation.6 | async-start | bytes 1966080 | tf_op jit(solution)/shard_map/all_to_all | solution.py:468
  240.6 1.0 copy-start.1
Sparse Core Ops, SparseCore 0:
  36.4 68.2 all-gather.2
  147.0 33.5 reduce-scatter.2
  183.3 27.7 reduce-scatter.4

commit v2 on v1

--- a/solution.py
+++ b/solution.py
@@ -457,8 +457,8 @@
     gq_got = lax.ppermute(gq_oth, "core", SWAP)
     gff_near = lax.psum_scatter(gff, "z")
     gx = lax.all_to_all(gx, Y, 0, 0)
-    gq_got, gx, dx1, dx2, gff_near = lax.optimization_barrier((gq_got, gx, dx1, dx2, gff_near))
     gq = (gq_own.astype(F32) + gq_got.astype(F32)).astype(BF)
+    gq, gx, dx1, dx2, gff_near = lax.optimization_barrier((gq, gx, dx1, dx2, gff_near))
 
     gq_near = lax.psum_scatter(gq, "z")
     gx = lax.all_to_all(gx.astype(F32).sum(0).astype(BF), NEAR_Y, 0, 0)

time: 251 us -> 249 us (level)
    all_to_all x1, waiting for transfers between devices: 9.31 us -> 6.73 us  [body(): gx = lax.all_to_all(gx, Y, 0, 0)]
  transfers between devices with their start and end apart: 18 -> 18, of which waited for: 13 -> 13; matrix products, arithmetic and copies ran while one was open for 8% -> 9% of each run, Pallas kernels for 9% -> 9%
where the time goes in v2:
time: 249 us; the launch traced here: 248 us
  waiting for transfers between devices  97.8 us (39%)
  starting transfers between devices  53.1 us (21%)
  Pallas kernels  44.4 us (18%)
  local copies, waits for them, and re-layouts  19.4 us (8%)
  other arithmetic  18.8 us (8%)
  between operations  14.3 us (6%)
    pallas_call x5, Pallas kernels, call(): pl.pallas_call(kernel, out_shape=[jax.ShapeDtypeStruct(shape, dtype) for...  44.4 us
    all_to_all x1, waiting for transfers between devices, body(): near = lax.all_to_all(to_all(flat, 8, 8), AXES, 0, 0)  28.3 us
    all_to_all x1, waiting for transfers between devices, body(): lax.all_to_all(jnp.concatenate([ff, pieces_of(gq_near, 7, 5)], axis=1), N...  14.8 us
    ppermute x4, waiting for transfers between devices, along(): lax.ppermute(v, SEQ, [(i - distance, i) for i in range(8) if 0 <= i - dis...  14.2 us
    all_to_all x1, waiting for transfers between devices, body(): near = lax.all_to_all(to_all(flat_ff, 2, 8), NEAR_Z, 0, 0)  10.7 us
    ppermute x4, starting transfers between devices, along(): lax.ppermute(v, SEQ, [(i - distance, i) for i in range(8) if 0 <= i - dis...  10.3 us
    all_to_all x1, starting transfers between devices, body(): lax.all_to_all(jnp.concatenate([ff, pieces_of(gq_near, 7, 5)], axis=1), N...  9.92 us
    all_to_all x1, starting transfers between devices, body(): near = lax.all_to_all(to_all(flat_ff, 2, 8), NEAR_Z, 0, 0)  8.59 us
  transfers between devices with their start and end apart: 18, of which 13 were waited for; matrix products, arithmetic and copies ran while one was open for 9% of the time, Pallas kernels for 9%

profile of v2, /device:TPU:1, one launch (start us, length us, event | category | flops | bytes accessed | tf_op | source)
XLA Modules:
  0.0 247.7 jit_solution(2124320884933881414)
XLA Ops:
  7.3 0.8 slice_bitcast_fusion.2
  8.1 0.8 copy.86
  8.9 0.8 copy.85
  9.8 1.0 broadcast_in_dim.6
  10.8 8.6 %all-to-all-start = ((bf16[32,104,128]{2,1,0:T(8,128)(2,1)}), bf16[32,104,128]{2,1,0:T(8,128)(2,1)S(1)}, u32[]{:S(2)}, u32[]{:S(2)}) async-start(bf16[32,104,128]{2,1,0:T(8,128)(2,1)} %bitcast.12), calls=%async_computation | async-start | bytes 1703936 | tf_op jit(solution)/shard_map/all_to_all | solution.py:409
  19.5 0.5 slice.40
  20.3 0.1 concatenate.22
  20.5 0.7 add_subtract_fusion
  21.2 2.5 %multiply_sine_fusion = (f32[768,128]{1,0:T(8,128)}, f32[768,128]{1,0:T(8,128)}) fusion(f32[128]{0:T(128)S(1)} %multiply_power_fusion, f32[768]{0:T(1024)S(1)} %fusion.1), kind=kLoop, calls=%fused_computation.6 | loop fusion | flops 98304 | bytes 790016 | tf_op jit(solution)/shard_map/sin | solution.py:400
  23.7 10.7 %all-to-all-done = bf16[32,104,128]{2,1,0:T(8,128)(2,1)S(1)} async-done(((bf16[32,104,128]{2,1,0:T(8,128)(2,1)}), bf16[32,104,128]{2,1,0:T(8,128)(2,1)S(1)}, u32[]{:S(2)}, u32[]{:S(2)}) %all-to-all-start) | async-done | bytes 852000 | tf_op jit(solution)/shard_map/all_to_all | solution.py:409
  34.6 0.2 copy.67
  34.8 0.1 reshape.223
  35.0 0.2 copy.69
  35.2 0.1 reshape.225
  35.3 1.0 pad_maximum_fusion.1
  36.3 2.0 broadcast_in_dim.8
  38.3 6.7 %all-to-all-start.1 = ((bf16[128,79,128]{2,1,0:T(8,128)(2,1)}), bf16[128,79,128]{2,1,0:T(8,128)(2,1)S(1)}, u32[]{:S(2)}, u32[]{:S(2)}) async-start(bf16[128,79,128]{2,1,0:T(8,128)(2,1)} %bitcast.79), calls=%async_computation.1 | async-start | bytes 5242880 | tf_op jit(solution)/shard_map/all_to_all | solution.py:415
  45.1 4.8 %collective-permute-start.1 = (bf16[256,640]{1,0:T(8,128)(2,1)S(1)}, bf16[256,640]{1,0:T(8,128)(2,1)S(1)}, u32[]{:S(2)}, u32[]{:S(2)}) collective-permute-start(bf16[256,640]{1,0:T(8,128)(2,1)S(1)} %bitcast.87), channel_id=1, source_target_pairs={{0,2},{1,3},{2,4},{3,5},{4,6},{5,7},{8,10},{9,11},{10,12},{11,13},... | collective-permute-start | bytes 983048 | tf_op jit(solution)/shard_map/ppermute | solution.py:392
  49.9 2.9 %collective-permute-start = (bf16[256,640]{1,0:T(8,128)(2,1)S(1)}, bf16[256,640]{1,0:T(8,128)(2,1)}, u32[]{:S(2)}, u32[]{:S(2)}) collective-permute-start(bf16[256,640]{1,0:T(8,128)(2,1)S(1)} %bitcast.88), channel_id=1, source_target_pairs={{0,1},{1,2},{2,3},{3,4},{4,5},{5,6},{6,7},{8,9},{9,10},{10,11},{11... | collective-permute-start | bytes 983048 | tf_op jit(solution)/shard_map/ppermute | solution.py:392
  52.8 28.3 %all-to-all-done.1 = bf16[128,79,128]{2,1,0:T(8,128)(2,1)S(1)} async-done(((bf16[128,79,128]{2,1,0:T(8,128)(2,1)}), bf16[128,79,128]{2,1,0:T(8,128)(2,1)S(1)}, u32[]{:S(2)}, u32[]{:S(2)}) %all-to-all-start.1) | async-done | bytes 2588704 | tf_op jit(solution)/shard_map/all_to_all | solution.py:415
  81.2 0.4 copy.70
  81.6 1.9 copy.71
  83.4 3.2 %reshape.228.own = bf16[3840,128]{1,0:T(8,128)(2,1)} reshape(bf16[6,128,5,128]{3,2,1,0:T(8,128)(2,1)} %copy.71) | data formatting | bytes 1966080 | tf_op jit(solution)/shard_map/reshape | solution.py:375
  86.6 5.7 %collective-permute-start.2 = (bf16[3840,128]{1,0:T(8,128)(2,1)}, bf16[3840,128]{1,0:T(8,128)(2,1)}, u32[]{:S(2)}, u32[]{:S(2)}) collective-permute-start(bf16[3840,128]{1,0:T(8,128)(2,1)} %reshape.228.own), channel_id=1, source_target_pairs={{0,8},{8,0},{1,9},{9,1},{2,10},{10,2},{3,11},{11,3},{4,12},{12,4},... | collective-permute-start | bytes 2949128 | tf_op jit(solution)/shard_map/ppermute | solution.py:418
  92.3 0.8 copy.72.pos_ref
  93.2 0.6 copy.84
  93.8 1.1 collective-permute-done.2.oth
  94.9 7.2 %attend.1 = (bf16[768,640]{1,0:T(8,128)(2,1)}, f32[4,256,256]{2,1,0:T(8,128)}, f32[768,256]{1,0:T(8,128)}, bf16[4,256,256]{2,1,0:T(8,128)(2,1)}, bf16[768,512]{1...) custom-call(s32[1]{0:T(128)} %bitcast.core_ref, ...), custom_call_target="tpu_custom_call" | custom-call | tf_op jit(solution)/shard_map/attend/pallas_call | solution.py:348
  102.1 2.6 %all-gather.3.cloned.1.call-done = bf16[13312,128]{1,0:T(8,128)(2,1)} async-done(((bf16[3328,128]{1,0:T(8,128)(2,1)}), bf16[13312,128]{1,0:T(8,128)(2,1)}) %all-gather.3.cloned.1.call-update) | async-done | bytes 3407888 | tf_op jit(solution)/shard_map/all_gather | solution.py:413
  104.7 0.5 collective-permute-start.3
  105.3 1.2 copy-done
  106.5 6.6 %collective-permute-done.4.down_oth = bf16[128,48,128]{2,1,0:T(8,128)(2,1)S(1)} collective-permute-done((bf16[128,48,128]{2,1,0:T(8,128)(2,1)S(1)}, bf16[128,48,128]{2,1,0:T(8,128)(2,1)S(1)}, u32[]{:S(2)}, u32[]{:S(2)}) %collective-permute-start.4) | collective-permute-done | bytes 1572896 | tf_op jit(solution)/shard_map/ppermute | solution.py:420
  113.1 1.2 copy-done.5
  114.2 19.0 %feed.1 = (bf16[256,640]{1,0:T(8,128)(2,1)}, f32[256,640]{1,0:T(8,128)}, bf16[4,256,256]{2,1,0:T(8,128)(2,1)}, f32[8,640]{1,0:T(8,128)}, bf16[4,2560,128]{2,1,0:...) custom-call(s32[1]{0:T(128)} %bitcast.core_ref, ...), custom_call_target="tpu_custom_call" | custom-call | tf_op jit(solution)/shard_map/feed/pallas_call | solution.py:348
  133.2 0.4 collective-permute-start.5
  133.6 0.3 collective-permute-start.6
  133.9 5.2 %collective-permute-done.5 = bf16[4,2560,128]{2,1,0:T(8,128)(2,1)S(1)} collective-permute-done((bf16[4,2560,128]{2,1,0:T(8,128)(2,1)}, bf16[4,2560,128]{2,1,0:T(8,128)(2,1)S(1)}, u32[]{:S(2)}, u32[]{:S(2)}) %collective-permute-start.5) | collective-permute-done | bytes 2621472 | tf_op jit(solution)/shard_map/ppermute | solution.py:439
  139.1 4.0 %add_convert_fusion = bf16[4,2560,128]{2,1,0:T(8,128)(2,1)} fusion(bf16[4,2560,128]{2,1,0:T(8,128)(2,1)S(1)} %collective-permute-done.5, bf16[4,2560,128]{2,1,0:T(8,128)(2,1)} %get-tuple-element.95), kind=kLoop, calls=%fused_computation | loop fusion | flops 5242880 | bytes 7864320 | tf_op jit(solution)/shard_map/convert_element_type | solution.py:439
  143.2 3.7 %add_convert_fusion.1 = bf16[4,32,72,128]{3,2,1,0:T(8,128)(2,1)} fusion(bf16[4,32,80,128]{3,2,1,0:T(8,128)(2,1)} %collective-permute-done.6, bf16[4,32,80,128]{3,2,1,0:T(8,128)(2,1)S(1)} %copy-done.4), kind=kLoop, calls=%fused_computation.1 | loop fusion | flops 4718592 | bytes 7077888 | tf_op jit(solution)/shard_map/convert_element_type | solution.py:439
  146.9 4.0 %all-to-all-start.2 = ((bf16[4,32,72,128]{3,2,1,0:T(8,128)(2,1)}), bf16[4,32,72,128]{3,2,1,0:T(8,128)(2,1)S(1)}, u32[]{:S(2)}, u32[]{:S(2)}) async-start(bf16[4,32,72,128]{3,2,1,0:T(8,128)(2,1)} %add_convert_fusion.1), calls=%async_computation.2 | async-start | bytes 4718592 | tf_op jit(solution)/shard_map/all_to_all | solution.py:459
  150.9 6.4 %attend_back.1 = (f32[4,256,256]{2,1,0:T(8,128)}, f32[768,512]{1,0:T(8,128)}) custom-call(bf16[4,256,256]{2,1,0:T(8,128)(2,1)} %get-tuple-element.91.q_ref, bf16[768,512]{1,0:T(8,128)(2,1)} %get-tuple-element.92.kv_ref, s32[256,1]{1,0:T(8,128)} %copy.72.pos_ref, f32[4,256,128]{2,1,0:T(8,128)} %get-tuple-element.93.log_ref, ...), custom_call_target="tpu_custom_call" | custom-call | tf_op jit(solution)/shard_map/attend_back/pallas_call | solution.py:348
  157.3 9.6 %project_back.1 = (f32[256,640]{1,0:T(8,128)}, bf16[256,640]{1,0:T(8,128)(2,1)}, bf16[256,640]{1,0:T(8,128)(2,1)}, bf16[4,1120,128]{2,1,0:T(8,128)(2,1)}, bf16[4,1120,128]{2,1,0:T(8,128)(2,1)}) custom-call(s32[1]{0:T(128)} %bitcast.core_ref, bf16[256,640]{1,0:T(8,128)(2,1)} %bitcast.86, bf16[256,640]{1,0:T(8,128)(2,1)} %collective-permute-done.x1, ...), custom_call_target="tpu_custom_call" | custom-call | tf_op jit(solution)/shard_map/project_back/pallas_call | solution.py:348
  166.9 0.7 collective-permute-start.7
  167.5 2.6 %collective-permute-done.7 = bf16[4,1120,128]{2,1,0:T(8,128)(2,1)S(1)} collective-permute-done((bf16[4,1120,128]{2,1,0:T(8,128)(2,1)}, bf16[4,1120,128]{2,1,0:T(8,128)(2,1)S(1)}, u32[]{:S(2)}, u32[]{:S(2)}) %collective-permute-start.7) | collective-permute-done | bytes 1146912 | tf_op jit(solution)/shard_map/ppermute | solution.py:457
  170.2 2.6 %add_convert_fusion.2 = bf16[4,1120,128]{2,1,0:T(8,128)(2,1)} fusion(bf16[4,1120,128]{2,1,0:T(8,128)(2,1)S(1)} %collective-permute-done.7, bf16[4,1120,128]{2,1,0:T(8,128)(2,1)} %get-tuple-element.104), kind=kLoop, calls=%fused_computation.2 | loop fusion | flops 2293760 | bytes 3440640 | tf_op jit(solution)/shard_map/convert_element_type | solution.py:460
  172.8 6.7 %all-to-all-done.2 = bf16[4,32,72,128]{3,2,1,0:T(8,128)(2,1)S(1)} async-done(((bf16[4,32,72,128]{3,2,1,0:T(8,128)(2,1)}), bf16[4,32,72,128]{3,2,1,0:T(8,128)(2,1)S(1)}, u32[]{:S(2)}, u32[]{:S(2)}) %all-to-all-start.2) | async-done | bytes 2359328 | tf_op jit(solution)/shard_map/all_to_all | solution.py:459
  179.5 1.1 reduce-scatter.3.cloned.1.call-done
  180.6 1.3 reduce_sum.12
  181.9 5.9 %all-to-all-start.3 = ((bf16[32,72,128]{2,1,0:T(8,128)(2,1)}), bf16[32,72,128]{2,1,0:T(8,128)(2,1)S(1)}, u32[]{:S(2)}, u32[]{:S(2)}) async-start(bf16[32,72,128]{2,1,0:T(8,128)(2,1)} %reduce_sum.12), calls=%async_computation.4 | async-start | bytes 1179648 | tf_op jit(solution)/shard_map/all_to_all | solution.py:464
  187.8 1.3 collective-permute-start.8
  189.1 1.3 collective-permute-start.9
  190.4 0.2 reshape.234
  190.8 12.7 %collective-permute-done.8 = bf16[256,640]{1,0:T(8,128)(2,1)S(1)} collective-permute-done((bf16[256,640]{1,0:T(8,128)(2,1)}, bf16[256,640]{1,0:T(8,128)(2,1)S(1)}, u32[]{:S(2)}, u32[]{:S(2)}) %collective-permute-start.8) | collective-permute-done | bytes 327712 | tf_op jit(solution)/shard_map/ppermute | solution.py:392
  203.5 1.5 collective-permute-done.9
  205.0 3.9 %reduce-scatter.5.cloned.1.call-done = bf16[1,1120,128]{2,1,0:T(8,128)(2,1)} async-done(((bf16[4,1120,128]{2,1,0:T(8,128)(2,1)}), bf16[1,1120,128]{2,1,0:T(8,128)(2,1)}) %reduce-scatter.5.cloned.1.call-update) | async-done | bytes 286736 | tf_op jit(solution)/shard_map/reduce_scatter | solution.py:463
  208.9 1.1 reshape.237
  210.0 0.1 copy.77
  210.1 0.3 copy.76
  210.4 1.1 pad_maximum_fusion
  211.5 9.9 %all-to-all-start.4 = ((bf16[32,115,128]{2,1,0:T(8,128)(2,1)}), bf16[32,115,128]{2,1,0:T(8,128)(2,1)S(1)}, u32[]{:S(2)}, u32[]{:S(2)}) async-start(bf16[32,115,128]{2,1,0:T(8,128)(2,1)} %pad_maximum_fusion), calls=%async_computation.6 | async-start | bytes 1966080 | tf_op jit(solution)/shard_map/all_to_all | solution.py:468
  221.4 1.8 fusion
  223.2 14.8 %all-to-all-done.4.rest_ref = bf16[32,115,128]{2,1,0:T(8,128)(2,1)S(1)} async-done(((bf16[32,115,128]{2,1,0:T(8,128)(2,1)}), bf16[32,115,128]{2,1,0:T(8,128)(2,1)S(1)}, u32[]{:S(2)}, u32[]{:S(2)}) %all-to-all-start.4) | async-done | bytes 942112 | tf_op jit(solution)/shard_map/all_to_all | solution.py:468
  238.0 1.0 copy-done.1
  239.0 2.2 finish.1
  (78 shorter events, 1.3 us)
Async XLA Ops:
  7.2 12.3 %copy-start.11 = (s32[1,256]{1,0:T(1,128)S(1)}, s32[1,256]{1,0:T(1,128)}, u32[]{:S(2)}) copy-start(s32[1,256]{1,0:T(1,128)} %param.19) | copy-start | bytes 3076
  7.2 12.8 %copy-start.10 = (bf16[5,1024]{1,0:T(8,128)(2,1)S(1)}, bf16[5,1024]{1,0:T(8,128)(2,1)}, u32[]{:S(2)}) copy-start(bf16[5,1024]{1,0:T(8,128)(2,1)} %param.20) | copy-start | bytes 30724
  7.2 12.8 %copy-start.9 = (bf16[16,640]{1,0:T(8,128)(2,1)S(1)}, bf16[16,640]{1,0:T(8,128)(2,1)}, u32[]{:S(2)}) copy-start(bf16[16,640]{1,0:T(8,128)(2,1)} %param.26) | copy-start | bytes 61444
  7.2 12.9 %copy-start.19 = (bf16[2]{0:T(256)(128)(2,1)S(1)}, bf16[2]{0:T(256)(128)(2,1)}, u32[]{:S(2)}) copy-start(bf16[2]{0:T(256)(128)(2,1)} %param.32) | copy-start | bytes 16
  7.2 12.9 %copy-start.18 = (bf16[2]{0:T(256)(128)(2,1)S(1)}, bf16[2]{0:T(256)(128)(2,1)}, u32[]{:S(2)}) copy-start(bf16[2]{0:T(256)(128)(2,1)} %param.31) | copy-start | bytes 16
  7.2 12.9 %copy-start.17 = (bf16[5]{0:T(256)(128)(2,1)S(1)}, bf16[5]{0:T(256)(128)(2,1)}, u32[]{:S(2)}) copy-start(bf16[5]{0:T(256)(128)(2,1)} %param.30) | copy-start | bytes 34
  7.2 12.9 %copy-start.16 = (bf16[5]{0:T(256)(128)(2,1)S(1)}, bf16[5]{0:T(256)(128)(2,1)}, u32[]{:S(2)}) copy-start(bf16[5]{0:T(256)(128)(2,1)} %param.29) | copy-start | bytes 34
  7.3 12.9 %copy-start.15 = (bf16[5]{0:T(256)(128)(2,1)S(1)}, bf16[5]{0:T(256)(128)(2,1)}, u32[]{:S(2)}) copy-start(bf16[5]{0:T(256)(128)(2,1)} %param.28) | copy-start | bytes 34
  7.3 12.9 %copy-start.14 = (bf16[5]{0:T(256)(128)(2,1)S(1)}, bf16[5]{0:T(256)(128)(2,1)}, u32[]{:S(2)}) copy-start(bf16[5]{0:T(256)(128)(2,1)} %param.27) | copy-start | bytes 34
  7.3 13.0 %copy-start.13 = (bf16[5,256]{1,0:T(8,128)(2,1)S(1)}, bf16[5,256]{1,0:T(8,128)(2,1)}, u32[]{:S(2)}) copy-start(bf16[5,256]{1,0:T(8,128)(2,1)} %param.22) | copy-start | bytes 7684
  7.3 13.0 %copy-start.12 = (bf16[5,256]{1,0:T(8,128)(2,1)S(1)}, bf16[5,256]{1,0:T(8,128)(2,1)}, u32[]{:S(2)}) copy-start(bf16[5,256]{1,0:T(8,128)(2,1)} %param.21) | copy-start | bytes 7684
  10.8 23.6 %all-to-all-start = ((bf16[32,104,128]{2,1,0:T(8,128)(2,1)}), bf16[32,104,128]{2,1,0:T(8,128)(2,1)S(1)}, u32[]{:S(2)}, u32[]{:S(2)}) async-start(bf16[32,104,128]{2,1,0:T(8,128)(2,1)} %bitcast.12), calls=%async_computation | async-start | bytes 1703936 | tf_op jit(solution)/shard_map/all_to_all | solution.py:409
  19.4 85.3 %all-gather.3.cloned.1.call-start = ((), (), s32[]{:S(2)}) async-start(), calls=%async_computation.9 | async-start | bytes 4259840 | tf_op jit(solution)/shard_map/all_gather | solution.py:413
  38.3 6.8 %copy-start.2 = (bf16[1,256,640]{2,1,0:T(8,128)(2,1)S(1)}, bf16[1,256,640]{2,1,0:T(8,128)(2,1)}, u32[]{:S(2)}) copy-start(bf16[1,256,640]{2,1,0:T(8,128)(2,1)} %param.18) | copy-start | bytes 983044
  38.3 42.8 %all-to-all-start.1 = ((bf16[128,79,128]{2,1,0:T(8,128)(2,1)}), bf16[128,79,128]{2,1,0:T(8,128)(2,1)S(1)}, u32[]{:S(2)}, u32[]{:S(2)}) async-start(bf16[128,79,128]{2,1,0:T(8,128)(2,1)} %bitcast.79), calls=%async_computation.1 | async-start | bytes 5242880 | tf_op jit(solution)/shard_map/all_to_all | solution.py:415
  45.0 135.5 %reduce-scatter.3.cloned.1.call-start = ((), (), s32[]{:S(2)}) async-start(), calls=%async_computation.7 | async-start | bytes 3276800 | tf_op jit(solution)/shard_map/reduce_scatter | solution.py:458
  45.1 41.5 %collective-permute-start.1 = (bf16[256,640]{1,0:T(8,128)(2,1)S(1)}, bf16[256,640]{1,0:T(8,128)(2,1)S(1)}, u32[]{:S(2)}, u32[]{:S(2)}) collective-permute-start(bf16[256,640]{1,0:T(8,128)(2,1)S(1)} %bitcast.87), channel_id=1, source_target_pairs={{0,2},{1,3},{2,4},{3,5},{4,6},{5,7},{8,10},{9,11},{10,12},{11,13},... | collective-permute-start | bytes 983048 | tf_op jit(solution)/shard_map/ppermute | solution.py:392
  49.9 36.7 %collective-permute-start = (bf16[256,640]{1,0:T(8,128)(2,1)S(1)}, bf16[256,640]{1,0:T(8,128)(2,1)}, u32[]{:S(2)}, u32[]{:S(2)}) collective-permute-start(bf16[256,640]{1,0:T(8,128)(2,1)S(1)} %bitcast.88), channel_id=1, source_target_pairs={{0,1},{1,2},{2,3},{3,4},{4,5},{5,6},{6,7},{8,9},{9,10},{10,11},{11... | collective-permute-start | bytes 983048 | tf_op jit(solution)/shard_map/ppermute | solution.py:392
  86.6 8.2 %copy-start.6 = (bf16[256,640]{1,0:T(8,128)(2,1)}, bf16[256,640]{1,0:T(8,128)(2,1)S(1)}, u32[]{:S(2)}) copy-start(bf16[256,640]{1,0:T(8,128)(2,1)S(1)} %collective-permute-done.1.x2) | copy-start | bytes 983044
  86.6 8.2 %collective-permute-start.2 = (bf16[3840,128]{1,0:T(8,128)(2,1)}, bf16[3840,128]{1,0:T(8,128)(2,1)}, u32[]{:S(2)}, u32[]{:S(2)}) collective-permute-start(bf16[3840,128]{1,0:T(8,128)(2,1)} %reshape.228.own), channel_id=1, source_target_pairs={{0,8},{8,0},{1,9},{9,1},{2,10},{10,2},{3,11},{11,3},{4,12},{12,4},... | collective-permute-start | bytes 2949128 | tf_op jit(solution)/shard_map/ppermute | solution.py:418
  104.7 8.4 %collective-permute-start.3 = (bf16[4,3328,128]{2,1,0:T(8,128)(2,1)}, bf16[4,3328,128]{2,1,0:T(8,128)(2,1)}, u32[]{:S(2)}, u32[]{:S(2)}) collective-permute-start(bf16[4,3328,128]{2,1,0:T(8,128)(2,1)} %bitcast.82), channel_id=1, source_target_pairs={{0,8},{8,0},{1,9},{9,1},{2,10},{10,2},{3,11},{11,3},{4,12},{12,4},... | collective-permute-start | bytes 10223624 | tf_op jit(solution)/shard_map/ppermute | solution.py:429
  105.3 1.2 copy-start
  106.4 6.6 %collective-permute-start.4 = (bf16[128,48,128]{2,1,0:T(8,128)(2,1)S(1)}, bf16[128,48,128]{2,1,0:T(8,128)(2,1)S(1)}, u32[]{:S(2)}, u32[]{:S(2)}) collective-permute-start(bf16[128,48,128]{2,1,0:T(8,128)(2,1)S(1)} %slice.54.down_own), channel_id=1, source_target_pairs={{0,8},{8,0},{1,9},{9,1},{2,10},{10,2},{3,11},{11,3},{4,12},{12,4},... | collective-permute-start | bytes 4718600 | tf_op jit(solution)/shard_map/ppermute | solution.py:420
  113.1 1.2 copy-start.5
  133.2 5.9 %collective-permute-start.5 = (bf16[4,2560,128]{2,1,0:T(8,128)(2,1)}, bf16[4,2560,128]{2,1,0:T(8,128)(2,1)S(1)}, u32[]{:S(2)}, u32[]{:S(2)}) collective-permute-start(bf16[4,2560,128]{2,1,0:T(8,128)(2,1)} %get-tuple-element.96), channel_id=1, source_target_pairs={{0,8},{8,0},{1,9},{9,1},{2,10},{10,2},{3,11},{11,3},{4,12},{12,4},... | collective-permute-start | bytes 7864328 | tf_op jit(solution)/shard_map/ppermute | solution.py:439
  133.6 9.6 %collective-permute-start.6 = (bf16[4,32,80,128]{3,2,1,0:T(8,128)(2,1)}, bf16[4,32,80,128]{3,2,1,0:T(8,128)(2,1)}, u32[]{:S(2)}, u32[]{:S(2)}) collective-permute-start(bf16[4,32,80,128]{3,2,1,0:T(8,128)(2,1)} %get-tuple-element.98), channel_id=1, source_target_pairs={{0,8},{8,0},{1,9},{9,1},{2,10},{10,2},{3,11},{11,3},{4,12},{12,4},... | collective-permute-start | bytes 7864328 | tf_op jit(solution)/shard_map/ppermute | solution.py:439
  139.1 4.0 %copy-start.4 = (bf16[4,32,80,128]{3,2,1,0:T(8,128)(2,1)S(1)}, bf16[4,32,80,128]{3,2,1,0:T(8,128)(2,1)}, u32[]{:S(2)}) copy-start(bf16[4,32,80,128]{3,2,1,0:T(8,128)(2,1)} %get-tuple-element.97) | copy-start | bytes 7864324
  146.9 32.6 %all-to-all-start.2 = ((bf16[4,32,72,128]{3,2,1,0:T(8,128)(2,1)}), bf16[4,32,72,128]{3,2,1,0:T(8,128)(2,1)S(1)}, u32[]{:S(2)}, u32[]{:S(2)}) async-start(bf16[4,32,72,128]{3,2,1,0:T(8,128)(2,1)} %add_convert_fusion.1), calls=%async_computation.2 | async-start | bytes 4718592 | tf_op jit(solution)/shard_map/all_to_all | solution.py:459
  150.9 58.0 %reduce-scatter.5.cloned.1.call-start = ((), (), s32[]{:S(2)}) async-start(), calls=%async_computation.8 | async-start | bytes 1433600 | tf_op jit(solution)/shard_map/reduce_scatter | solution.py:463
  166.9 3.3 %collective-permute-start.7 = (bf16[4,1120,128]{2,1,0:T(8,128)(2,1)}, bf16[4,1120,128]{2,1,0:T(8,128)(2,1)S(1)}, u32[]{:S(2)}, u32[]{:S(2)}) collective-permute-start(bf16[4,1120,128]{2,1,0:T(8,128)(2,1)} %get-tuple-element.105), channel_id=1, source_target_pairs={{0,8},{8,0},{1,9},{9,1},{2,10},{10,2},{3,11},{11,3},{4,12},{12,4},... | collective-permute-start | bytes 3440648 | tf_op jit(solution)/shard_map/ppermute | solution.py:457
  180.6 9.9 %copy-start.8 = (bf16[1,2560,128]{2,1,0:T(8,128)(2,1)S(1)}, bf16[1,2560,128]{2,1,0:T(8,128)(2,1)}, u32[]{:S(2)}) copy-start(bf16[1,2560,128]{2,1,0:T(8,128)(2,1)} %reduce-scatter.3.cloned.1.call-done) | copy-start | bytes 1966084
  181.9 23.1 %all-to-all-start.3 = ((bf16[32,72,128]{2,1,0:T(8,128)(2,1)}), bf16[32,72,128]{2,1,0:T(8,128)(2,1)S(1)}, u32[]{:S(2)}, u32[]{:S(2)}) async-start(bf16[32,72,128]{2,1,0:T(8,128)(2,1)} %reduce_sum.12), calls=%async_computation.4 | async-start | bytes 1179648 | tf_op jit(solution)/shard_map/all_to_all | solution.py:464
  187.8 15.7 %collective-permute-start.8 = (bf16[256,640]{1,0:T(8,128)(2,1)}, bf16[256,640]{1,0:T(8,128)(2,1)S(1)}, u32[]{:S(2)}, u32[]{:S(2)}) collective-permute-start(bf16[256,640]{1,0:T(8,128)(2,1)} %get-tuple-element.111), channel_id=1, source_target_pairs={{1,0},{2,1},{3,2},{4,3},{5,4},{6,5},{7,6},{9,8},{10,9},{11,10},{12... | collective-permute-start | bytes 983048 | tf_op jit(solution)/shard_map/ppermute | solution.py:392
  189.1 15.9 %collective-permute-start.9 = (bf16[256,640]{1,0:T(8,128)(2,1)}, bf16[256,640]{1,0:T(8,128)(2,1)}, u32[]{:S(2)}, u32[]{:S(2)}) collective-permute-start(bf16[256,640]{1,0:T(8,128)(2,1)} %get-tuple-element.112), channel_id=1, source_target_pairs={{2,0},{3,1},{4,2},{5,3},{6,4},{7,5},{10,8},{11,9},{12,10},{13,11},... | collective-permute-start | bytes 983048 | tf_op jit(solution)/shard_map/ppermute | solution.py:392
  205.0 6.4 %copy-start.3 = (bf16[32,72,128]{2,1,0:T(8,128)(2,1)}, bf16[32,72,128]{2,1,0:T(8,128)(2,1)S(1)}, u32[]{:S(2)}) copy-start(bf16[32,72,128]{2,1,0:T(8,128)(2,1)S(1)} %all-to-all-done.3.gx_ref) | copy-start | bytes 1769476
  210.1 11.3 %copy-start.7 = (f32[256,640]{1,0:T(8,128)S(1)}, f32[256,640]{1,0:T(8,128)}, u32[]{:S(2)}) copy-start(f32[256,640]{1,0:T(8,128)} %get-tuple-element.103) | copy-start | bytes 1966084
  211.5 26.5 %all-to-all-start.4 = ((bf16[32,115,128]{2,1,0:T(8,128)(2,1)}), bf16[32,115,128]{2,1,0:T(8,128)(2,1)S(1)}, u32[]{:S(2)}, u32[]{:S(2)}) async-start(bf16[32,115,128]{2,1,0:T(8,128)(2,1)} %pad_maximum_fusion), calls=%async_computation.6 | async-start | bytes 1966080 | tf_op jit(solution)/shard_map/all_to_all | solution.py:468
  238.0 1.0 copy-start.1
Sparse Core Ops, SparseCore 0:
  36.4 68.2 all-gather.2
  147.0 33.5 reduce-scatter.2
  183.0 25.8 reduce-scatter.4
